TPU v7x, 1024 devices: a whole 4x4x32 slice. The times are simulated.
1024 devices in a mesh: rep: 8 (over x, core), shard: 128 (over z, y).
Axes of the slice: x: 4, y: 4, z: 32, core: 2. Of those that a mesh axis runs over, the one named last changes fastest.
Arguments:
- partial_grads: bfloat16 [8, 8, 7168, 576], P('rep', None, 'shard'), may hold values from -1440 to 1440
- momentum: float32 [8, 7168, 576], P('rep', 'shard'), may hold values from -6 to 6
Outputs:
- update: bfloat16 [8, 7168, 576], P(None, 'shard')
- new_momentum: float32 [8, 7168, 576], P('rep', 'shard')
All inputs are finite; a program needn't handle non-finite values.
Results may differ from a plain program's by a relative error of at most 0.0056.
The roundings to bfloat16 on the way count: a program that leaves them out, or rounds other values in their place, can miss the bound.
Values may be sent and summed in bfloat16 or wider, within the bound.
No kernel may reach another device: no remote copies, remote signals or barrier semaphores. Data moves between devices by JAX's collectives and lax.ppermute only.
A program may use at most 32 MiB of HBM per device.

v0:
```python
import math

import jax
import jax.numpy as jnp
from jax import lax
from jax.sharding import PartitionSpec as P

ITERS = 2


linear_coeff = 3.4445
cubic_coeff = -4.775
quintic_coeff = 2.0315
momentum_rate = 0.9
norm_eps = 1e-06


def local(partial_grads, momentum):
    summed = lax.psum_scatter(
        partial_grads.astype(jnp.float32), "rep", scatter_dimension=1, tiled=True
    )[0]
    new_momentum = momentum_rate * momentum + summed
    current = (summed + momentum_rate * new_momentum).astype(jnp.bfloat16)
    matrix_count, row_count, kv_width = current.shape
    shard_count = lax.axis_size("shard")
    factor = 0.2 * math.sqrt(max(row_count * shard_count, kv_width))
    padded_width = -(-kv_width // shard_count) * shard_count
    totals = lax.psum(jnp.sum(jnp.square(current.astype(jnp.float32)), axis=(1, 2)), "shard")
    inv_norm = 1.0 / (jnp.sqrt(totals) + norm_eps)
    for iteration in range(ITERS):
        padded_current = jnp.pad(current, ((0, 0), (0, 0), (0, padded_width - kv_width)))
        slices = lax.psum_scatter(
            jnp.einsum("mrk,mrl->kml", padded_current, current, preferred_element_type=jnp.float32),
            "shard",
            scatter_dimension=0,
            tiled=True,
        )
        if iteration == 0:
            slices = slices * (inv_norm * inv_norm)[None, :, None]
        gathered = lax.all_gather(slices.astype(jnp.bfloat16), "shard", axis=0, tiled=True)
        gram_b = jnp.transpose(gathered[:kv_width], (1, 0, 2))
        gram_b = lax.optimization_barrier(gram_b)
        squared = jnp.einsum("mkl,mln->mkn", gram_b, gram_b, preferred_element_type=jnp.float32)
        poly_term = (cubic_coeff * gram_b.astype(jnp.float32) + quintic_coeff * squared).astype(
            jnp.bfloat16
        )
        next_iter = linear_coeff * current.astype(jnp.float32) + jnp.einsum(
            "mrk,mkl->mrl", current, poly_term, preferred_element_type=jnp.float32
        )
        if iteration == 0:
            next_iter = next_iter * inv_norm[:, None, None]
        if iteration == ITERS - 1:
            next_iter = next_iter * factor
        current = next_iter.astype(jnp.bfloat16)
    update = lax.all_gather(current, "rep", axis=0, tiled=True)
    return (update, new_momentum)


def solution(mesh):
    placed = (P("rep", None, "shard", None), P("rep", "shard", None))
    return jax.shard_map(
        local,
        mesh=mesh,
        in_specs=placed,
        out_specs=(P(None, "shard", None), P("rep", "shard", None)),
        check_vma=False,
    )
```

profile of v0, /device:TPU:1, one launch (start us, length us, event | category | flops | bytes accessed | tf_op | source)
XLA Modules:
  0.0 1681.5 jit_solution(11603990450646760536)
XLA Ops:
  7.2 0.0 copy-start
  7.2 0.0 reduce-scatter.5.cloned.1.call-start
  7.2 2.2 convert_element_type.40
  9.4 0.0 reduce-scatter.5.cloned.1.call-update
  9.4 0.0 all-reduce.8.cloned.1.call-start
  9.5 60.0 %reduce-scatter.5.cloned.1.call-done = f32[1,1,56,576]{3,2,1,0:T(8,128)} async-done(((f32[1,8,56,576]{3,2,1,0:T(8,128)}), f32[1,1,56,576]{3,2,1,0:T(8,128)}) %reduce-scatter.5.cloned.1.call-update) | async-done | bytes 129040
  69.5 0.0 copy-done
  69.5 2.2 fusion.18
  71.7 0.4 convolution_bitcast_fusion.1
  72.1 2.8 copy.6
  74.8 0.0 all-reduce.8.cloned.1.call-update
  74.9 1.3 dynamic-slice.2
  76.7 226.0 %psum.7 = f32[1]{0:T(128)} all-reduce(f32[1]{0:T(128)} %bitcast.5), channel_id=1, replica_groups=mesh['rep'=8,'shard'=128] {'shard'}, use_global_device_ids=true, to_apply=%region_3.4 | all-reduce | flops 1 | bytes 8 | tf_op jit(solution)/shard_map/psum | solution.py:28
  303.4 263.8 %all-reduce.8.cloned.1.call-done = f32[640,1,576]{2,1,0:T(1,128)} async-done(((f32[640,1,576]{2,1,0:T(1,128)}), f32[640,1,576]{2,1,0:T(1,128)}) %all-reduce.8.cloned.1.call-update) | async-done | bytes 1474576
  567.2 0.7 fusion.28
  567.9 148.5 %all_gather.9 = bf16[640,1,576]{2,1,0:T(2,128)(2,1)S(1)} all-gather(bf16[5,1,576]{2,1,0:T(2,128)(2,1)S(1)} %fusion.28), channel_id=1, replica_groups=mesh['rep'=8,'shard'=128] {'shard'}, dimensions={0}, use_global_device_ids=true | all-gather | bytes 743040 | tf_op jit(solution)/shard_map/all_gather | solution.py:40
  716.4 1.5 slice.8
  718.0 0.1 copy.17
  718.1 1.1 fusion.8
  719.2 0.4 convolution_bitcast_fusion
  719.6 1.2 copy.8
  720.8 567.9 %all-reduce.9 = bf16[640,1,576]{2,1,0:T(2,128)(2,1)S(1)} all-reduce(f32[640,1,576]{2,1,0:T(1,128)S(1)} %copy.8), channel_id=4, replica_groups=mesh['rep'=8,'shard'=128] {'shard'}, use_global_device_ids=true, to_apply=%region_4.5.clone | all-reduce | flops 368640 | bytes 2211840
  1288.7 156.5 %all_gather.10 = bf16[640,1,576]{2,1,0:T(2,128)(2,1)S(1)} all-gather(bf16[5,1,576]{2,1,0:T(2,128)(2,1)S(1)} %dynamic-slice_convert_fusion), channel_id=1, replica_groups=mesh['rep'=8,'shard'=128] {'shard'}, dimensions={0}, use_global_device_ids=true | all-gather | bytes 743040 | tf_op jit(solution)/shard_map/all_gather | solution.py:40
  1445.2 1.5 slice.9
  1446.8 0.1 copy.16
  1446.9 1.1 fusion.9
  1448.0 225.9 %all_gather.11 = bf16[8,56,576]{2,1,0:T(8,128)(2,1)S(1)} all-gather(bf16[1,56,576]{2,1,0:T(8,128)(2,1)S(1)} %fusion.9), channel_id=1, replica_groups=mesh['rep'=8,'shard'=128] {'rep'}, dimensions={0}, use_global_device_ids=true | all-gather | bytes 580608 | tf_op jit(solution)/shard_map/all_gather | solution.py:55
  1673.9 0.8 copy.22
  (1 shorter events, 0.0 us)
Async XLA Ops:
  7.2 62.3 %copy-start = (f32[1,56,576]{2,1,0:T(8,128)S(1)}, f32[1,56,576]{2,1,0:T(8,128)}, u32[]{:S(2)}) copy-start(f32[1,56,576]{2,1,0:T(8,128)} %param.3) | copy-start | bytes 387076
  7.2 62.3 %reduce-scatter.5.cloned.1.call-start = ((), (), s32[]{:S(2)}) async-start(), calls=%async_computation.2 | async-start | bytes 1290240
  9.4 557.8 %all-reduce.8.cloned.1.call-start = ((), (), s32[]{:S(2)}) async-start(), calls=%async_computation.1 | async-start | bytes 3276800
Sparse Core Ops, SparseCore 0:
  11.4 58.0 reduce-scatter.4
  75.0 492.1 all-reduce.7
where the time goes:
time: 1680 us
  blocking collectives  1320 us (79%)
  waiting for transfers between devices  324 us (19%)
    unnamed x1, blocking collectives  568 us
    unnamed x4, waiting for transfers between devices  324 us
    all_gather x2, blocking collectives, local(): lax.all_gather(slices.astype(jnp.bfloat16), 'shard', axis=0, tiled=True)  305 us
    psum x1, blocking collectives, local(): lax.psum(jnp.sum(jnp.square(current.astype(jnp.float32)), axis=(1, 2)), '...  226 us
    all_gather x1, blocking collectives, local(): update = lax.all_gather(current, 'rep', axis=0, tiled=True)  226 us
  transfers between devices with their start and end apart: 2, of which 2 were waited for; matrix products, arithmetic and copies ran while one was open for 0% of the time, Pallas kernels for 0%

commit v1 on v0

v1 whole, which is shorter than its diff:
```python
import functools
import math

import jax
import jax.numpy as jnp
import numpy as np
from jax import lax
from jax.experimental import pallas as pl
from jax.experimental.pallas import tpu as pltpu
from jax.sharding import Mesh
from jax.sharding import PartitionSpec as P

linear_coeff = 3.4445
cubic_coeff = -4.775
quintic_coeff = 2.0315
momentum_rate = 0.9
norm_eps = 1e-06

TILE = 128
TILES = 5
WIDE = TILE * TILES
SLOTS = 4


def slot_tiles(y):
    return [
        (y, 4),
        (y, y),
        (y, (y + 1) % 4),
        [(0, 2), (1, 3), (4, 4), None][y],
    ]


def dot_tn(a, b):
    return lax.dot_general(a, b, (((0,), (0,)), ((), ())), preferred_element_type=jnp.float32)


def gram_kernel(rows_ref, out_ref):
    y = lax.axis_index("y")
    last = jnp.where(y < 2, y, 4)
    left = [y, y, y, last]
    right = [4, y, lax.rem(y + 1, 4), jnp.where(y < 2, y + 2, 4)]
    for slot in range(SLOTS):
        at = pl.ds(pl.multiple_of(left[slot] * TILE, TILE), TILE)
        to = pl.ds(pl.multiple_of(right[slot] * TILE, TILE), TILE)
        total = dot_tn(rows_ref[0, :, at], rows_ref[0, :, to])
        for part in range(1, rows_ref.shape[0]):
            total += dot_tn(rows_ref[part, :, at], rows_ref[part, :, to])
        tile = total.astype(out_ref.dtype)
        height = out_ref.shape[1]
        per = TILE // height
        for piece in range(per):
            out_ref[slot * per + piece] = tile[piece * height : (piece + 1) * height]


def sum_kernel(parts_ref, out_ref):
    total = parts_ref[0].astype(jnp.float32)
    for part in range(1, parts_ref.shape[0]):
        total += parts_ref[part].astype(jnp.float32)
    rounded = total.astype(out_ref.dtype)
    for part in range(out_ref.shape[0]):
        out_ref[part] = rounded


def newton_kernel(factor, tiles_ref, rows_ref, out_ref, gram, work, poly):
    total = jnp.float32(0.0)
    row = lax.broadcasted_iota(jnp.int32, (TILE, TILE), 0)
    col = lax.broadcasted_iota(jnp.int32, (TILE, TILE), 1)
    for y in range(4):
        for slot, place in enumerate(slot_tiles(y)):
            if place is None:
                continue
            i, j = place
            tile = tiles_ref[y, slot * TILE : (slot + 1) * TILE, :]
            gram[i * TILE : (i + 1) * TILE, j * TILE : (j + 1) * TILE] = tile
            wide = tile.astype(jnp.float32)
            if i == j:
                total += jnp.sum(jnp.where(row == col, wide, 0.0))
            else:
                gram[j * TILE : (j + 1) * TILE, i * TILE : (i + 1) * TILE] = wide.T.astype(gram.dtype)
    total = jnp.full((1, 1), total, jnp.float32)
    inv_norm = 1.0 / (jnp.sqrt(total) + norm_eps)
    inv_square = inv_norm * inv_norm

    def dot(a, b):
        return jnp.dot(a, b, preferred_element_type=jnp.float32)

    g = gram[...]
    square = dot(g, g) * inv_square
    poly[...] = (
        (cubic_coeff * g.astype(jnp.float32) + quintic_coeff * square) * inv_square
    ).astype(poly.dtype)
    half = (linear_coeff * g.astype(jnp.float32) + dot(g, poly[...])) * inv_square
    work[...] = half.astype(work.dtype)
    second = (linear_coeff * half + dot(poly[...], work[...])).astype(gram.dtype)

    rows = rows_ref[...]
    first = (linear_coeff * rows.astype(jnp.float32) + dot(rows, poly[...])) * inv_norm
    first = first.astype(jnp.bfloat16)

    gram[...] = second
    g = gram[...]
    work[...] = (
        cubic_coeff * g.astype(jnp.float32) + quintic_coeff * dot(g, g)
    ).astype(work.dtype)
    result = linear_coeff * first.astype(jnp.float32) + dot(first, work[...])
    out_ref[...] = (result * factor)[:, : out_ref.shape[1]].astype(out_ref.dtype)


def vmem(n):
    return [pl.BlockSpec(memory_space=pltpu.VMEM)] * n


def call(kernel, out, n_in, scratch=()):
    return pl.pallas_call(
        kernel,
        out_shape=jax.ShapeDtypeStruct(out, jnp.bfloat16),
        in_specs=vmem(n_in),
        out_specs=vmem(1)[0],
        scratch_shapes=[pltpu.VMEM(s, jnp.bfloat16) for s in scratch],
        compiler_params=pltpu.CompilerParams(vmem_limit_bytes=32 * 1024 * 1024),
    )


def local(partial_grads, momentum):
    rep = ("x", "core")
    planes, lanes = lax.axis_size("z"), lax.axis_size("y")
    received = lax.all_to_all(partial_grads[0], rep, 0, 0, tiled=True)
    summed = jnp.sum(received.astype(jnp.float32), axis=0)
    new_momentum = momentum_rate * momentum[0] + summed
    velocity = (summed + momentum_rate * new_momentum).astype(jnp.bfloat16)
    row_count, kv_width = velocity.shape
    factor = 0.2 * math.sqrt(max(row_count * planes * lanes, kv_width))

    wide = jnp.pad(velocity, ((0, 0), (0, WIDE - kv_width)))
    spread = jnp.broadcast_to(wide[None], (lanes, row_count, WIDE))
    plane_rows = lax.all_to_all(spread, "y", 0, 0, tiled=True)

    chunk = (planes, SLOTS * TILE // planes, TILE)
    parts = call(gram_kernel, chunk, 1)(plane_rows)
    parts = lax.all_to_all(parts, "z", 0, 0, tiled=True)
    shares = call(sum_kernel, chunk, 1)(parts)
    shares = lax.all_to_all(shares, "z", 0, 0, tiled=True)
    quarter = shares.reshape(SLOTS * TILE, TILE)
    quarters = lax.all_to_all(
        jnp.broadcast_to(quarter[None], (lanes, SLOTS * TILE, TILE)), "y", 0, 0, tiled=True
    )
    update = call(
        functools.partial(newton_kernel, factor), (row_count, kv_width), 2, [(WIDE, WIDE)] * 3
    )(quarters, wide)
    update = lax.all_gather(update, rep, axis=0, tiled=False)
    return (update, new_momentum[None])


def solution(mesh):
    devices = np.asarray(mesh.devices)
    fine = Mesh(devices.reshape(4, 2, 32, 4), ("x", "core", "z", "y"))
    rep, shard = ("x", "core"), ("z", "y")
    return jax.shard_map(
        local,
        mesh=fine,
        in_specs=(P(rep, None, shard, None), P(rep, shard, None)),
        out_specs=(P(None, shard, None), P(rep, shard, None)),
        check_vma=False,
    )
```

time: 1680 us -> 152 us (0.09)
  blocking collectives: 1320 us -> 133 us
  waiting for transfers between devices: 324 us -> 6.21 us
    unnamed x1 -> x0, blocking collectives: 568 us -> none
    all_gather x3 -> x1, blocking collectives: 531 us -> 19.5 us  [local(): update = lax.all_gather(update, rep, axis=0, tiled=False)]
    unnamed x4 -> x0, waiting for transfers between devices: 324 us -> none
    psum x1 -> x0, blocking collectives: 226 us -> none  [local(): lax.psum(jnp.sum(jnp.square(current.astype(jnp.float32)), axis=(1, 2)), '...]
    all_to_all x0 -> x4, blocking collectives: none -> 114 us  [the longest x1 44.8 us: local(): parts = lax.all_to_all(parts, 'z', 0, 0, tiled=True)]
  transfers between devices with their start and end apart: 2 -> 1, of which waited for: 2 -> 1; matrix products, arithmetic and copies ran while one was open for 0% -> 0% of each run, Pallas kernels for 0% -> 0%
where the time goes in v1:
time: 152 us; the launch traced here: 151 us
  blocking collectives  133 us (88%)
  waiting for transfers between devices  6.21 us (4%)
  Pallas kernels  4.09 us (3%)
  starting transfers between devices  3.47 us (2%)
  local copies, waits for them, and re-layouts  2.53 us (2%)
    all_to_all x1, blocking collectives, local(): parts = lax.all_to_all(parts, 'z', 0, 0, tiled=True)  44.8 us
    all_to_all x1, blocking collectives, local(): shares = lax.all_to_all(shares, 'z', 0, 0, tiled=True)  32.5 us
    all_to_all x1, blocking collectives, local(): received = lax.all_to_all(partial_grads[0], rep, 0, 0, tiled=True)  27.9 us
    all_gather x1, blocking collectives, local(): update = lax.all_gather(update, rep, axis=0, tiled=False)  19.5 us
    all_to_all x1, blocking collectives, local(): plane_rows = lax.all_to_all(spread, 'y', 0, 0, tiled=True)  8.71 us
    all_to_all x1, waiting for transfers between devices, local(): lax.all_to_all(jnp.broadcast_to(quarter[None], (lanes, SLOTS * TILE, TILE...  6.21 us
    pallas_call x1, Pallas kernels, local(): call(functools.partial(newton_kernel, factor), (row_count, kv_width), 2,...  3.71 us
    all_to_all x1, starting transfers between devices, local(): lax.all_to_all(jnp.broadcast_to(quarter[None], (lanes, SLOTS * TILE, TILE...  3.47 us
  transfers between devices with their start and end apart: 1, of which 1 were waited for; matrix products, arithmetic and copies ran while one was open for 0% of the time, Pallas kernels for 0%

profile of v1, /device:TPU:1, one launch (start us, length us, event | category | flops | bytes accessed | tf_op | source)
XLA Modules:
  0.0 151.2 jit_solution(16683062332209182849)
XLA Ops:
  0.6 27.9 %all_to_all.25 = bf16[8,56,576]{2,1,0:T(8,128)(2,1)S(1)} all-to-all(bf16[8,56,576]{2,1,0:T(8,128)(2,1)} %bitcast.14), channel_id=1, replica_groups=mesh['x'=4,'core'=2,'z'=32,'y'=4] {'x','core'}, dimensions={0} | all-to-all | bytes 1032192 | tf_op jit(solution)/shard_map/all_to_all | solution.py:128
  28.5 0.0 copy-start
  28.5 0.1 convert_reduce_fusion
  28.6 0.8 copy-done
  29.5 8.7 %all_to_all.26.rows_ref = bf16[4,56,640]{2,1,0:T(8,128)(2,1)S(1)} all-to-all(bf16[4,56,640]{2,1,0:T(8,128)(2,1)S(1)} %broadcast_in_dim.6), channel_id=1, replica_groups=mesh['x'=4,'core'=2,'z'=32,'y'=4] {'y'}, dimensions={0} | all-to-all | bytes 573440 | tf_op jit(solution)/shard_map/all_to_all | solution.py:137
  38.2 0.3 shard_map.41
  38.6 44.8 %all_to_all.27.parts_ref = bf16[32,16,128]{2,1,0:T(8,128)(2,1)S(1)} all-to-all(bf16[32,16,128]{2,1,0:T(8,128)(2,1)S(1)} %shard_map.41), channel_id=1, replica_groups=mesh['x'=4,'core'=2,'z'=32,'y'=4] {'z'}, dimensions={0} | all-to-all | bytes 262144 | tf_op jit(solution)/shard_map/all_to_all | solution.py:141
  83.4 32.5 %all_to_all.28 = bf16[32,16,128]{2,1,0:T(8,128)(2,1)S(1)} all-to-all(bf16[32,16,128]{2,1,0:T(8,128)(2,1)S(1)} %shard_map.42), channel_id=1, replica_groups=mesh['x'=4,'core'=2,'z'=32,'y'=4] {'z'}, dimensions={0} | all-to-all | bytes 262144 | tf_op jit(solution)/shard_map/all_to_all | solution.py:143
  115.9 0.9 broadcast_in_dim.16
  116.8 3.5 %all-to-all-start.4 = ((bf16[4,512,128]{2,1,0:T(8,128)(2,1)}), bf16[4,512,128]{2,1,0:T(8,128)(2,1)S(1)}, u32[]{:S(2)}, u32[]{:S(2)}) async-start(bf16[4,512,128]{2,1,0:T(8,128)(2,1)} %broadcast_in_dim.16), calls=%async_computation.4 | async-start | bytes 1048576 | tf_op jit(solution)/shard_map/all_to_all | solution.py:145
  120.3 0.7 bitcast_add_fusion
  121.0 6.2 %all-to-all-done.4.tiles_ref = bf16[4,512,128]{2,1,0:T(8,128)(2,1)S(1)} async-done(((bf16[4,512,128]{2,1,0:T(8,128)(2,1)}), bf16[4,512,128]{2,1,0:T(8,128)(2,1)S(1)}, u32[]{:S(2)}, u32[]{:S(2)}) %all-to-all-start.4) | async-done | bytes 524320 | tf_op jit(solution)/shard_map/all_to_all | solution.py:145
  127.2 3.7 %shard_map.43 = bf16[56,576]{1,0:T(8,128)(2,1)S(1)} custom-call(bf16[4,512,128]{2,1,0:T(8,128)(2,1)S(1)} %all-to-all-done.4.tiles_ref, bf16[56,640]{1,0:T(8,128)(2,1)S(1)} %pad.4.rows_ref), custom_call_target="tpu_custom_call" | custom-call | tf_op jit(solution)/shard_map/pallas_call | solution.py:148
  130.9 19.5 %all-gather = bf16[448,576]{1,0:T(8,128)(2,1)S(1)} all-gather(bf16[56,576]{1,0:T(8,128)(2,1)S(1)} %shard_map.43), channel_id=2, replica_groups=mesh['x'=4,'core'=2,'z'=32,'y'=4] {'x','core'}, dimensions={0}, use_global_device_ids=true | all-gather | bytes 580608 | tf_op jit(solution)/shard_map/all_gather | solution.py:151
  150.3 0.8 copy.5
  (4 shorter events, 0.1 us)
Async XLA Ops:
  28.5 0.9 copy-start
  116.8 10.4 %all-to-all-start.4 = ((bf16[4,512,128]{2,1,0:T(8,128)(2,1)}), bf16[4,512,128]{2,1,0:T(8,128)(2,1)S(1)}, u32[]{:S(2)}, u32[]{:S(2)}) async-start(bf16[4,512,128]{2,1,0:T(8,128)(2,1)} %broadcast_in_dim.16), calls=%async_computation.4 | async-start | bytes 1048576 | tf_op jit(solution)/shard_map/all_to_all | solution.py:145

commit v2 on v1

v2 whole, which is shorter than its diff:
```python
import functools
import math

import jax
import jax.numpy as jnp
import numpy as np
from jax import lax
from jax.experimental import pallas as pl
from jax.experimental.pallas import tpu as pltpu
from jax.sharding import Mesh
from jax.sharding import PartitionSpec as P

linear_coeff = 3.4445
cubic_coeff = -4.775
quintic_coeff = 2.0315
momentum_rate = 0.9
norm_eps = 1e-06

TILE = 128
HALF = 64
TILES = 5
WIDE = TILE * TILES
PACKED = 384


def dot_tn(a, b):
    return lax.dot_general(a, b, (((0,), (0,)), ((), ())), preferred_element_type=jnp.float32)


def left_half(rows):
    return lax.broadcasted_iota(jnp.int32, (rows, TILE), 1) < HALF


def gram_kernel(rows_ref, out_ref):
    y = lax.axis_index("y")

    def tile(i, j):
        at = pl.ds(pl.multiple_of(i * TILE, TILE), TILE)
        to = pl.ds(pl.multiple_of(j * TILE, TILE), TILE)
        total = dot_tn(rows_ref[0, :, at], rows_ref[0, :, to])
        for part in range(1, rows_ref.shape[0]):
            total += dot_tn(rows_ref[part, :, at], rows_ref[part, :, to])
        return total

    far = lax.rem(y, 2)
    split = tile(far, far + 2)
    diagonal = tile(y, y)
    out_ref[0:128, :] = tile(y, lax.rem(y + 1, 4)).astype(out_ref.dtype)
    out_ref[128:192, :] = jnp.where(y < 2, split[:HALF], split[HALF:]).astype(out_ref.dtype)
    out_ref[192:256, :] = tile(4, y)[:HALF].astype(out_ref.dtype)
    out_ref[256:320, :] = diagonal[:HALF].astype(out_ref.dtype)
    corner = jnp.where(left_half(HALF), tile(4, 4)[:HALF], diagonal[HALF:])
    out_ref[320:384, :] = corner.astype(out_ref.dtype)


def sum_kernel(parts_ref, out_ref):
    total = parts_ref[0].astype(jnp.float32)
    for part in range(1, parts_ref.shape[0]):
        total += parts_ref[part].astype(jnp.float32)
    rounded = total.astype(out_ref.dtype)
    for part in range(out_ref.shape[0]):
        out_ref[part] = rounded


def newton_kernel(factor, packed_ref, rows_ref, out_ref, gram, work, poly):
    zeros = jnp.zeros((HALF, TILE), jnp.float32)
    row = lax.broadcasted_iota(jnp.int32, (HALF, TILE), 0)
    col = lax.broadcasted_iota(jnp.int32, (HALF, TILE), 1)
    trace = zeros

    def part(y, start, stop):
        return packed_ref[y, start:stop, :].astype(jnp.float32)

    def put(i, j, tile):
        gram[i * TILE : (i + 1) * TILE, j * TILE : (j + 1) * TILE] = tile.astype(gram.dtype)

    def put_both(i, j, tile):
        put(i, j, tile)
        put(j, i, tile.T)

    for y in range(4):
        put_both(y, (y + 1) % 4, part(y, 0, 128))
        put_both(4, y, jnp.concatenate([part(y, 192, 256), zeros], axis=0))
        upper, corner = part(y, 256, 320), part(y, 320, 384)
        mirrored = jnp.concatenate([upper, zeros], axis=0).T
        lower = jnp.where(left_half(HALF), mirrored[HALF:], corner)
        put(y, y, jnp.concatenate([upper, lower], axis=0))
        trace += jnp.where(row == col, upper, 0.0) + jnp.where(row + HALF == col, corner, 0.0)
        if y == 0:
            trace += jnp.where(row == col, corner, 0.0)
            last = jnp.where(left_half(HALF), corner, 0.0)
            put(4, 4, jnp.concatenate([last, zeros], axis=0))
    for i in range(2):
        put_both(i, i + 2, jnp.concatenate([part(i, 128, 192), part(i + 2, 128, 192)], axis=0))

    total = jnp.sum(trace, axis=(0, 1), keepdims=True)
    inv_norm = 1.0 / (jnp.sqrt(total) + norm_eps)
    inv_square = inv_norm * inv_norm

    def dot(a, b):
        return jnp.dot(a, b, preferred_element_type=jnp.float32)

    g = gram[...]
    square = dot(g, g) * inv_square
    poly[...] = (
        (cubic_coeff * g.astype(jnp.float32) + quintic_coeff * square) * inv_square
    ).astype(poly.dtype)
    half = (linear_coeff * g.astype(jnp.float32) + dot(g, poly[...])) * inv_square
    work[...] = half.astype(work.dtype)
    second = (linear_coeff * half + dot(poly[...], work[...])).astype(gram.dtype)

    rows = rows_ref[...]
    first = (linear_coeff * rows.astype(jnp.float32) + dot(rows, poly[...])) * inv_norm
    first = first.astype(jnp.bfloat16)

    gram[...] = second
    g = gram[...]
    work[...] = (
        cubic_coeff * g.astype(jnp.float32) + quintic_coeff * dot(g, g)
    ).astype(work.dtype)
    result = linear_coeff * first.astype(jnp.float32) + dot(first, work[...])
    out_ref[...] = (result * factor)[:, : out_ref.shape[1]].astype(out_ref.dtype)


def vmem(n):
    return [pl.BlockSpec(memory_space=pltpu.VMEM)] * n


def call(kernel, out, n_in, scratch=()):
    return pl.pallas_call(
        kernel,
        out_shape=jax.ShapeDtypeStruct(out, jnp.bfloat16),
        in_specs=vmem(n_in),
        out_specs=vmem(1)[0],
        scratch_shapes=[pltpu.VMEM(s, jnp.bfloat16) for s in scratch],
        compiler_params=pltpu.CompilerParams(vmem_limit_bytes=32 * 1024 * 1024),
    )


def local(partial_grads, momentum):
    rep = ("x", "core")
    lanes, blocks, near = lax.axis_size("y"), lax.axis_size("block"), lax.axis_size("near")
    received = lax.all_to_all(partial_grads[0], rep, 0, 0, tiled=True)
    summed = jnp.sum(received.astype(jnp.float32), axis=0)
    new_momentum = momentum_rate * momentum[0] + summed
    velocity = (summed + momentum_rate * new_momentum).astype(jnp.bfloat16)
    row_count, kv_width = velocity.shape
    factor = 0.2 * math.sqrt(max(row_count * blocks * near * lanes, kv_width))

    wide = jnp.pad(velocity, ((0, 0), (0, WIDE - kv_width)))
    spread = jnp.broadcast_to(wide[None], (lanes, row_count, WIDE))
    plane_rows = lax.all_to_all(spread, "y", 0, 0, tiled=True)

    share = PACKED // near
    parts = call(gram_kernel, (PACKED, TILE), 1)(plane_rows).reshape(near, share, TILE)
    parts = lax.all_to_all(parts, "near", 0, 0, tiled=True)
    parts = call(sum_kernel, (blocks, share, TILE), 1)(parts)
    parts = lax.all_to_all(parts, "block", 0, 0, tiled=True)
    parts = call(sum_kernel, (near, share, TILE), 1)(parts)
    parts = lax.all_to_all(parts, "near", 0, 0, tiled=True)
    packed = jnp.broadcast_to(parts.reshape(1, PACKED, TILE), (lanes, PACKED, TILE))
    packed = lax.all_to_all(packed, "y", 0, 0, tiled=True)
    update = call(
        functools.partial(newton_kernel, factor), (row_count, kv_width), 2, [(WIDE, WIDE)] * 3
    )(packed, wide)
    update = lax.all_gather(update, rep, axis=0, tiled=False)
    return (update, new_momentum[None])


def solution(mesh):
    devices = np.asarray(mesh.devices)
    fine = Mesh(devices.reshape(4, 2, 4, 8, 4), ("x", "core", "block", "near", "y"))
    rep, shard = ("x", "core"), ("block", "near", "y")
    return jax.shard_map(
        local,
        mesh=fine,
        in_specs=(P(rep, None, shard, None), P(rep, shard, None)),
        out_specs=(P(None, shard, None), P(rep, shard, None)),
        check_vma=False,
    )
```

time: 152 us -> 140 us (0.921)
  blocking collectives: 133 us -> 123 us
    all_to_all x2 -> x3, blocking collectives: 77.3 us -> 65.8 us  [the longest x1 40.6 us: local(): parts = lax.all_to_all(parts, 'block', 0, 0, tiled=True)]
where the time goes in v2:
time: 140 us
  blocking collectives  123 us (88%)
  waiting for transfers between devices  5.51 us (4%)
  Pallas kernels  4.11 us (3%)
  starting transfers between devices  3.46 us (2%)
  local copies, waits for them, and re-layouts  2.46 us (2%)
    all_to_all x1, blocking collectives, local(): parts = lax.all_to_all(parts, 'block', 0, 0, tiled=True)  40.6 us
    all_to_all x1, blocking collectives, local(): received = lax.all_to_all(partial_grads[0], rep, 0, 0, tiled=True)  27.9 us
    all_to_all x2, blocking collectives, local(): parts = lax.all_to_all(parts, 'near', 0, 0, tiled=True)  25.2 us
    all_gather x1, blocking collectives, local(): update = lax.all_gather(update, rep, axis=0, tiled=False)  20.4 us
    all_to_all x1, blocking collectives, local(): plane_rows = lax.all_to_all(spread, 'y', 0, 0, tiled=True)  8.71 us
    all_to_all x1, waiting for transfers between devices, local(): packed = lax.all_to_all(packed, 'y', 0, 0, tiled=True)  5.51 us
    pallas_call x1, Pallas kernels, local(): call(functools.partial(newton_kernel, factor), (row_count, kv_width), 2,...  3.71 us
    all_to_all x1, starting transfers between devices, local(): packed = lax.all_to_all(packed, 'y', 0, 0, tiled=True)  3.46 us
  transfers between devices with their start and end apart: 1, of which 1 were waited for; matrix products, arithmetic and copies ran while one was open for 0% of the time, Pallas kernels for 0%

profile of v2, /device:TPU:1, one launch (start us, length us, event | category | flops | bytes accessed | tf_op | source)
XLA Modules:
  0.0 139.9 jit_solution(8670284154203733071)
XLA Ops:
  0.6 27.9 %all_to_all.30 = bf16[8,56,576]{2,1,0:T(8,128)(2,1)S(1)} all-to-all(bf16[8,56,576]{2,1,0:T(8,128)(2,1)} %bitcast.16), channel_id=1, replica_groups=mesh['x'=4,'core'=2,'block'=4,'near'=8,'y'=4] {'x','core'}, dimensions={0} | all-to-all | bytes 1032192 | tf_op jit(solution)/shard_map/all_to_all | solution.py:143
  28.5 0.0 copy-start
  28.5 0.1 convert_reduce_fusion
  28.6 0.8 copy-done
  29.5 8.7 %all_to_all.31.rows_ref = bf16[4,56,640]{2,1,0:T(8,128)(2,1)S(1)} all-to-all(bf16[4,56,640]{2,1,0:T(8,128)(2,1)S(1)} %broadcast_in_dim.6), channel_id=1, replica_groups=mesh['x'=4,'core'=2,'block'=4,'near'=8,'y'=4] {'y'}, dimensions={0} | all-to-all | bytes 573440 | tf_op jit(solution)/shard_map/all_to_all | solution.py:152
  38.2 0.4 shard_map.41
  38.6 12.4 %all_to_all.32.parts_ref = bf16[8,48,128]{2,1,0:T(8,128)(2,1)S(1)} all-to-all(bf16[8,48,128]{2,1,0:T(8,128)(2,1)S(1)} %bitcast.14), channel_id=1, replica_groups=mesh['x'=4,'core'=2,'block'=4,'near'=8,'y'=4] {'near'}, dimensions={0} | all-to-all | bytes 196608 | tf_op jit(solution)/shard_map/all_to_all | solution.py:156
  51.0 40.6 %all_to_all.33.parts_ref = bf16[4,48,128]{2,1,0:T(8,128)(2,1)S(1)} all-to-all(bf16[4,48,128]{2,1,0:T(8,128)(2,1)S(1)} %shard_map.42), channel_id=1, replica_groups=mesh['x'=4,'core'=2,'block'=4,'near'=8,'y'=4] {'block'}, dimensions={0} | all-to-all | bytes 98304 | tf_op jit(solution)/shard_map/all_to_all | solution.py:158
  91.6 12.8 %all_to_all.34 = bf16[8,48,128]{2,1,0:T(8,128)(2,1)S(1)} all-to-all(bf16[8,48,128]{2,1,0:T(8,128)(2,1)S(1)} %shard_map.43), channel_id=1, replica_groups=mesh['x'=4,'core'=2,'block'=4,'near'=8,'y'=4] {'near'}, dimensions={0} | all-to-all | bytes 196608 | tf_op jit(solution)/shard_map/all_to_all | solution.py:160
  104.4 0.8 broadcast_in_dim.16
  105.2 3.5 %all-to-all-start.5 = ((bf16[4,384,128]{2,1,0:T(8,128)(2,1)}), bf16[4,384,128]{2,1,0:T(8,128)(2,1)S(1)}, u32[]{:S(2)}, u32[]{:S(2)}) async-start(bf16[4,384,128]{2,1,0:T(8,128)(2,1)} %broadcast_in_dim.16), calls=%async_computation.5 | async-start | bytes 786432 | tf_op jit(solution)/shard_map/all_to_all | solution.py:162
  108.7 0.7 bitcast_add_fusion
  109.4 5.5 %all-to-all-done.5.packed_ref = bf16[4,384,128]{2,1,0:T(8,128)(2,1)S(1)} async-done(((bf16[4,384,128]{2,1,0:T(8,128)(2,1)}), bf16[4,384,128]{2,1,0:T(8,128)(2,1)S(1)}, u32[]{:S(2)}, u32[]{:S(2)}) %all-to-all-start.5) | async-done | bytes 393248 | tf_op jit(solution)/shard_map/all_to_all | solution.py:162
  114.9 3.7 %shard_map.44 = bf16[56,576]{1,0:T(8,128)(2,1)S(1)} custom-call(bf16[4,384,128]{2,1,0:T(8,128)(2,1)S(1)} %all-to-all-done.5.packed_ref, bf16[56,640]{1,0:T(8,128)(2,1)S(1)} %pad.4.rows_ref), custom_call_target="tpu_custom_call" | custom-call | tf_op jit(solution)/shard_map/pallas_call | solution.py:163
  118.6 20.4 %all-gather = bf16[448,576]{1,0:T(8,128)(2,1)S(1)} all-gather(bf16[56,576]{1,0:T(8,128)(2,1)S(1)} %shard_map.44), channel_id=2, replica_groups=mesh['x'=4,'core'=2,'block'=4,'near'=8,'y'=4] {'x','core'}, dimensions={0}, use_global_device_ids=true | all-gather | bytes 580608 | tf_op jit(solution)/shard_map/all_gather | solution.py:166
  139.1 0.8 copy.5
  (5 shorter events, 0.1 us)
Async XLA Ops:
  28.5 0.9 copy-start
  105.2 9.7 %all-to-all-start.5 = ((bf16[4,384,128]{2,1,0:T(8,128)(2,1)}), bf16[4,384,128]{2,1,0:T(8,128)(2,1)S(1)}, u32[]{:S(2)}, u32[]{:S(2)}) async-start(bf16[4,384,128]{2,1,0:T(8,128)(2,1)} %broadcast_in_dim.16), calls=%async_computation.5 | async-start | bytes 786432 | tf_op jit(solution)/shard_map/all_to_all | solution.py:162

commit v3 on v2

v3 whole, which is shorter than its diff:
```python
import functools
import math

import jax
import jax.numpy as jnp
import numpy as np
from jax import lax
from jax.experimental import pallas as pl
from jax.experimental.pallas import tpu as pltpu
from jax.sharding import Mesh
from jax.sharding import PartitionSpec as P

linear_coeff = 3.4445
cubic_coeff = -4.775
quintic_coeff = 2.0315
momentum_rate = 0.9
norm_eps = 1e-06

TILE = 128
HALF = 64
TILES = 5
WIDE = TILE * TILES
GROUPS = 4
PACKED = 384


def left_half(rows):
    return lax.broadcasted_iota(jnp.int32, (rows, TILE), 1) < HALF


def gram_kernel(
    received_ref, momentum_ref, wide_ref, packed_ref, new_ref, momentum, new, read_done, write_done
):
    read = pltpu.make_async_copy(momentum_ref, momentum, read_done)
    read.start()
    summed = received_ref[0].astype(jnp.float32)
    for part in range(1, received_ref.shape[0]):
        summed += received_ref[part].astype(jnp.float32)
    read.wait()
    updated = momentum_rate * momentum[...] + summed
    new[...] = updated
    write = pltpu.make_async_copy(new, new_ref, write_done)
    write.start()
    velocity = (summed + momentum_rate * updated).astype(wide_ref.dtype)
    rows, width = velocity.shape
    padding = jnp.zeros((rows, WIDE - width), wide_ref.dtype)
    wide_ref[...] = jnp.concatenate([velocity, padding], axis=1)

    def tile(i, j):
        return lax.dot_general(
            wide_ref[:, i * TILE : (i + 1) * TILE],
            wide_ref[:, j * TILE : (j + 1) * TILE],
            (((0,), (0,)), ((), ())),
            preferred_element_type=jnp.float32,
        )

    def put(start, block):
        packed_ref[start : start + block.shape[0], :] = block.astype(packed_ref.dtype)

    last = tile(4, 4)[:HALF]
    for y in range(GROUPS):
        base = y * PACKED
        put(base, tile(y, (y + 1) % 4))
        put(base + 192, tile(4, y)[:HALF])
        diagonal = tile(y, y)
        put(base + 256, diagonal[:HALF])
        put(base + 320, jnp.where(left_half(HALF), last, diagonal[HALF:]))
    for i in range(2):
        split = tile(i, i + 2)
        put(i * PACKED + 128, split[:HALF])
        put((i + 2) * PACKED + 128, split[HALF:])
    write.wait()


def sum_kernel(parts_ref, out_ref):
    total = parts_ref[0].astype(jnp.float32)
    for part in range(1, parts_ref.shape[0]):
        total += parts_ref[part].astype(jnp.float32)
    rounded = total.astype(out_ref.dtype)
    for part in range(out_ref.shape[0]):
        out_ref[part] = rounded


def newton_kernel(factor, packed_ref, rows_ref, out_ref, gram, work, poly):
    zeros = jnp.zeros((HALF, TILE), jnp.float32)
    row = lax.broadcasted_iota(jnp.int32, (HALF, TILE), 0)
    col = lax.broadcasted_iota(jnp.int32, (HALF, TILE), 1)
    trace = zeros

    def part(y, start, stop):
        return packed_ref[y * PACKED + start : y * PACKED + stop, :].astype(jnp.float32)

    def put(i, j, tile):
        gram[i * TILE : (i + 1) * TILE, j * TILE : (j + 1) * TILE] = tile.astype(gram.dtype)

    def put_both(i, j, tile):
        put(i, j, tile)
        put(j, i, tile.T)

    for y in range(GROUPS):
        put_both(y, (y + 1) % 4, part(y, 0, 128))
        put_both(4, y, jnp.concatenate([part(y, 192, 256), zeros], axis=0))
        upper, corner = part(y, 256, 320), part(y, 320, 384)
        mirrored = jnp.concatenate([upper, zeros], axis=0).T
        lower = jnp.where(left_half(HALF), mirrored[HALF:], corner)
        put(y, y, jnp.concatenate([upper, lower], axis=0))
        trace += jnp.where(row == col, upper, 0.0) + jnp.where(row + HALF == col, corner, 0.0)
        if y == 0:
            trace += jnp.where(row == col, corner, 0.0)
            last = jnp.where(left_half(HALF), corner, 0.0)
            put(4, 4, jnp.concatenate([last, zeros], axis=0))
    for i in range(2):
        put_both(i, i + 2, jnp.concatenate([part(i, 128, 192), part(i + 2, 128, 192)], axis=0))

    total = jnp.sum(trace, axis=(0, 1), keepdims=True)
    inv_norm = 1.0 / (jnp.sqrt(total) + norm_eps)
    inv_square = inv_norm * inv_norm

    def dot(a, b):
        return jnp.dot(a, b, preferred_element_type=jnp.float32)

    g = gram[...]
    square = dot(g, g) * inv_square
    poly[...] = (
        (cubic_coeff * g.astype(jnp.float32) + quintic_coeff * square) * inv_square
    ).astype(poly.dtype)
    half = (linear_coeff * g.astype(jnp.float32) + dot(g, poly[...])) * inv_square
    work[...] = half.astype(work.dtype)
    second = (linear_coeff * half + dot(poly[...], work[...])).astype(gram.dtype)

    rows = rows_ref[...]
    first = (linear_coeff * rows.astype(jnp.float32) + dot(rows, poly[...])) * inv_norm
    first = first.astype(jnp.bfloat16)

    gram[...] = second
    g = gram[...]
    work[...] = (
        cubic_coeff * g.astype(jnp.float32) + quintic_coeff * dot(g, g)
    ).astype(work.dtype)
    result = linear_coeff * first.astype(jnp.float32) + dot(first, work[...])
    out_ref[...] = (result * factor)[:, : out_ref.shape[1]].astype(out_ref.dtype)


VMEM = pl.BlockSpec(memory_space=pltpu.VMEM)
HBM = pl.BlockSpec(memory_space=pl.ANY)
PARAMS = pltpu.CompilerParams(vmem_limit_bytes=32 * 1024 * 1024)


def bf16(*shape):
    return jax.ShapeDtypeStruct(shape, jnp.bfloat16)


def gram(received, momentum):
    rows = momentum.shape[0]
    return pl.pallas_call(
        gram_kernel,
        out_shape=(
            bf16(rows, WIDE),
            bf16(GROUPS * PACKED, TILE),
            jax.ShapeDtypeStruct(momentum.shape, momentum.dtype),
        ),
        in_specs=[VMEM, HBM],
        out_specs=(VMEM, VMEM, HBM),
        scratch_shapes=[pltpu.VMEM(momentum.shape, momentum.dtype)] * 2
        + [pltpu.SemaphoreType.DMA] * 2,
        compiler_params=PARAMS,
    )(received, momentum)


def total_of(parts, receivers):
    return pl.pallas_call(
        sum_kernel,
        out_shape=bf16(receivers, *parts.shape[1:]),
        in_specs=[VMEM],
        out_specs=VMEM,
        compiler_params=PARAMS,
    )(parts)


def newton(factor, packed, wide, width):
    return pl.pallas_call(
        functools.partial(newton_kernel, factor),
        out_shape=bf16(wide.shape[0], width),
        in_specs=[VMEM, VMEM],
        out_specs=VMEM,
        scratch_shapes=[pltpu.VMEM((WIDE, WIDE), jnp.bfloat16)] * 3,
        compiler_params=PARAMS,
    )(packed, wide)


def local(partial_grads, momentum):
    rep, cluster = ("x", "core"), ("near", "y")
    blocks = lax.axis_size("block")
    members = lax.axis_size(cluster)
    row_count, kv_width = momentum.shape[1:]
    factor = 0.2 * math.sqrt(max(row_count * blocks * members, kv_width))

    received = lax.all_to_all(partial_grads[0], rep, 0, 0, tiled=True)
    wide, packed, new_momentum = gram(received, momentum[0])

    packed = packed.reshape(members, GROUPS * PACKED // members, TILE)
    packed = lax.all_to_all(packed, cluster, 0, 0, tiled=True)
    packed = lax.all_to_all(total_of(packed, blocks), "block", 0, 0, tiled=True)
    packed = lax.all_to_all(total_of(packed, members), cluster, 0, 0, tiled=True)
    packed = packed.reshape(GROUPS * PACKED, TILE)

    update = newton(factor, packed, wide, kv_width)
    update = lax.all_gather(update, rep, axis=0, tiled=False)
    return (update, new_momentum[None])


def solution(mesh):
    devices = np.asarray(mesh.devices)
    fine = Mesh(devices.reshape(4, 2, 8, 4, 4), ("x", "core", "block", "near", "y"))
    rep, shard = ("x", "core"), ("block", "near", "y")
    return jax.shard_map(
        local,
        mesh=fine,
        in_specs=(P(rep, None, shard, None), P(rep, shard, None)),
        out_specs=(P(None, shard, None), P(rep, shard, None)),
        check_vma=False,
    )
```

time: 140 us -> 132 us (0.943)
  waiting for transfers between devices: 5.51 us -> 0 us
  starting transfers between devices: 3.46 us -> 0 us
  blocking collectives: 123 us -> 126 us
  local copies, waits for them, and re-layouts: 2.46 us -> 0.81 us
    all_to_all x4 -> x3, blocking collectives: 74.5 us -> 80.8 us  [the longest x1 48.1 us: local(): packed = lax.all_to_all(total_of(packed, blocks), 'block', 0, 0, tiled=True)]
    all_to_all x1 -> x0, waiting for transfers between devices: 5.51 us -> none  [local(): packed = lax.all_to_all(packed, 'y', 0, 0, tiled=True)]
    all_to_all x1 -> x0, starting transfers between devices: 3.46 us -> none  [local(): packed = lax.all_to_all(packed, 'y', 0, 0, tiled=True)]
    all_gather x1, blocking collectives: 20.4 us -> 17.1 us  [local(): update = lax.all_gather(update, rep, axis=0, tiled=False)]
  transfers between devices with their start and end apart: 1 -> 0, of which waited for: 1 -> 0; matrix products, arithmetic and copies ran while one was open for 0% -> 0% of each run, Pallas kernels for 0% -> 0%
where the time goes in v3:
time: 132 us
  blocking collectives  126 us (95%)
  Pallas kernels  4.76 us (4%)
    all_to_all x1, blocking collectives, local(): packed = lax.all_to_all(total_of(packed, blocks), 'block', 0, 0, tiled=True)  48.1 us
    all_to_all x1, blocking collectives, local(): received = lax.all_to_all(partial_grads[0], rep, 0, 0, tiled=True)  28 us
    all_to_all x1, blocking collectives, local(): lax.all_to_all(total_of(packed, members), cluster, 0, 0, tiled=True)  18.1 us
    all_gather x1, blocking collectives, local(): update = lax.all_gather(update, rep, axis=0, tiled=False)  17.1 us
    all_to_all x1, blocking collectives, local(): packed = lax.all_to_all(packed, cluster, 0, 0, tiled=True)  14.5 us
    pallas_call x1, Pallas kernels, newton(): pl.pallas_call(functools.partial(newton_kernel, factor), out_shape=bf16(w...  3.71 us

profile of v3, /device:TPU:1, one launch (start us, length us, event | category | flops | bytes accessed | tf_op | source)
XLA Modules:
  0.0 132.2 jit_solution(6638691805309076141)
XLA Ops:
  0.6 0.0 copy-start
  0.6 28.0 %all_to_all.20.received_ref = bf16[8,56,576]{2,1,0:T(8,128)(2,1)S(1)} all-to-all(bf16[8,56,576]{2,1,0:T(8,128)(2,1)} %bitcast.10), channel_id=1, replica_groups=mesh['x'=4,'core'=2,'block'=8,'near'=4,'y'=4] {'x','core'}, dimensions={0} | all-to-all | bytes 1032192 | tf_op jit(solution)/shard_map/all_to_all | solution.py:198
  28.6 0.0 copy-done
  28.6 0.9 shard_map.41
  29.6 14.5 %all_to_all.21.parts_ref = bf16[16,96,128]{2,1,0:T(8,128)(2,1)S(1)} all-to-all(bf16[16,96,128]{2,1,0:T(8,128)(2,1)S(1)} %bitcast.7), channel_id=1, replica_groups=mesh['x'=4,'core'=2,'block'=8,'near'=4,'y'=4] {'near','y'}, dimensions={0} | all-to-all | bytes 786432 | tf_op jit(solution)/shard_map/all_to_all | solution.py:202
  44.1 0.1 shard_map.42
  44.2 48.1 %all_to_all.22.parts_ref = bf16[8,96,128]{2,1,0:T(8,128)(2,1)S(1)} all-to-all(bf16[8,96,128]{2,1,0:T(8,128)(2,1)S(1)} %shard_map.42), channel_id=1, replica_groups=mesh['x'=4,'core'=2,'block'=8,'near'=4,'y'=4] {'block'}, dimensions={0} | all-to-all | bytes 393216 | tf_op jit(solution)/shard_map/all_to_all | solution.py:203
  92.3 18.1 %all_to_all.23 = bf16[16,96,128]{2,1,0:T(8,128)(2,1)S(1)} all-to-all(bf16[16,96,128]{2,1,0:T(8,128)(2,1)S(1)} %shard_map.43), channel_id=1, replica_groups=mesh['x'=4,'core'=2,'block'=8,'near'=4,'y'=4] {'near','y'}, dimensions={0} | all-to-all | bytes 786432 | tf_op jit(solution)/shard_map/all_to_all | solution.py:204
  110.5 3.7 %shard_map.44 = bf16[56,576]{1,0:T(8,128)(2,1)S(1)} custom-call(bf16[1536,128]{1,0:T(8,128)(2,1)S(1)} %bitcast.6, bf16[56,640]{1,0:T(8,128)(2,1)S(1)} %get-tuple-element.6.rows_ref), custom_call_target="tpu_custom_call" | custom-call | tf_op jit(solution)/shard_map/pallas_call | solution.py:181
  114.2 17.1 %all-gather = bf16[448,576]{1,0:T(8,128)(2,1)S(1)} all-gather(bf16[56,576]{1,0:T(8,128)(2,1)S(1)} %shard_map.44), channel_id=2, replica_groups=mesh['x'=4,'core'=2,'block'=8,'near'=4,'y'=4] {'x','core'}, dimensions={0}, use_global_device_ids=true | all-gather | bytes 580608 | tf_op jit(solution)/shard_map/all_gather | solution.py:208
  131.4 0.8 copy.5
  (1 shorter events, 0.0 us)
Async XLA Ops:
  0.6 28.0 %copy-start = (f32[1,56,576]{2,1,0:T(8,128)S(1)}, f32[1,56,576]{2,1,0:T(8,128)}, u32[]{:S(2)}) copy-start(f32[1,56,576]{2,1,0:T(8,128)} %param.3) | copy-start | bytes 387076

commit v4 on v3

--- a/solution.py
+++ b/solution.py
@@ -211,7 +211,7 @@
 
 def solution(mesh):
     devices = np.asarray(mesh.devices)
-    fine = Mesh(devices.reshape(4, 2, 8, 4, 4), ("x", "core", "block", "near", "y"))
+    fine = Mesh(devices.reshape(4, 2, 4, 8, 4), ("x", "core", "block", "near", "y"))
     rep, shard = ("x", "core"), ("block", "near", "y")
     return jax.shard_map(
         local,

time: 132 us -> 148 us (1.12)
  blocking collectives: 126 us -> 141 us
    all_to_all x1, blocking collectives: 18.1 us -> 29.4 us  [local(): lax.all_to_all(total_of(packed, members), cluster, 0, 0, tiled=True)]
    all_to_all x1, blocking collectives: 14.5 us -> 23.4 us  [local(): packed = lax.all_to_all(packed, cluster, 0, 0, tiled=True)]
    all_to_all x1, blocking collectives: 48.1 us -> 42.2 us  [local(): packed = lax.all_to_all(total_of(packed, blocks), 'block', 0, 0, tiled=True)]
where the time goes in v4:
time: 148 us
  blocking collectives  141 us (95%)
  Pallas kernels  4.76 us (3%)
    all_to_all x1, blocking collectives, local(): packed = lax.all_to_all(total_of(packed, blocks), 'block', 0, 0, tiled=True)  42.2 us
    all_to_all x1, blocking collectives, local(): lax.all_to_all(total_of(packed, members), cluster, 0, 0, tiled=True)  29.4 us
    all_to_all x1, blocking collectives, local(): received = lax.all_to_all(partial_grads[0], rep, 0, 0, tiled=True)  28 us
    all_to_all x1, blocking collectives, local(): packed = lax.all_to_all(packed, cluster, 0, 0, tiled=True)  23.4 us
    all_gather x1, blocking collectives, local(): update = lax.all_gather(update, rep, axis=0, tiled=False)  18.3 us
    pallas_call x1, Pallas kernels, newton(): pl.pallas_call(functools.partial(newton_kernel, factor), out_shape=bf16(w...  3.72 us

profile of v4, /device:TPU:1, one launch (start us, length us, event | category | flops | bytes accessed | tf_op | source)
XLA Modules:
  0.0 147.5 jit_solution(7349424168878442669)
XLA Ops:
  0.6 0.0 copy-start
  0.6 28.0 %all_to_all.20.received_ref = bf16[8,56,576]{2,1,0:T(8,128)(2,1)S(1)} all-to-all(bf16[8,56,576]{2,1,0:T(8,128)(2,1)} %bitcast.10), channel_id=1, replica_groups=mesh['x'=4,'core'=2,'block'=4,'near'=8,'y'=4] {'x','core'}, dimensions={0} | all-to-all | bytes 1032192 | tf_op jit(solution)/shard_map/all_to_all | solution.py:198
  28.6 0.0 copy-done
  28.6 0.9 shard_map.41
  29.6 23.4 %all_to_all.21.parts_ref = bf16[32,48,128]{2,1,0:T(8,128)(2,1)S(1)} all-to-all(bf16[32,48,128]{2,1,0:T(8,128)(2,1)S(1)} %bitcast.7), channel_id=1, replica_groups=mesh['x'=4,'core'=2,'block'=4,'near'=8,'y'=4] {'near','y'}, dimensions={0} | all-to-all | bytes 786432 | tf_op jit(solution)/shard_map/all_to_all | solution.py:202
  53.0 0.1 shard_map.42
  53.1 42.2 %all_to_all.22.parts_ref = bf16[4,48,128]{2,1,0:T(8,128)(2,1)S(1)} all-to-all(bf16[4,48,128]{2,1,0:T(8,128)(2,1)S(1)} %shard_map.42), channel_id=1, replica_groups=mesh['x'=4,'core'=2,'block'=4,'near'=8,'y'=4] {'block'}, dimensions={0} | all-to-all | bytes 98304 | tf_op jit(solution)/shard_map/all_to_all | solution.py:203
  95.3 29.4 %all_to_all.23 = bf16[32,48,128]{2,1,0:T(8,128)(2,1)S(1)} all-to-all(bf16[32,48,128]{2,1,0:T(8,128)(2,1)S(1)} %shard_map.43), channel_id=1, replica_groups=mesh['x'=4,'core'=2,'block'=4,'near'=8,'y'=4] {'near','y'}, dimensions={0} | all-to-all | bytes 786432 | tf_op jit(solution)/shard_map/all_to_all | solution.py:204
  124.7 3.7 %shard_map.44 = bf16[56,576]{1,0:T(8,128)(2,1)S(1)} custom-call(bf16[1536,128]{1,0:T(8,128)(2,1)S(1)} %bitcast.6, bf16[56,640]{1,0:T(8,128)(2,1)S(1)} %get-tuple-element.6.rows_ref), custom_call_target="tpu_custom_call" | custom-call | tf_op jit(solution)/shard_map/pallas_call | solution.py:181
  128.4 18.3 %all-gather = bf16[448,576]{1,0:T(8,128)(2,1)S(1)} all-gather(bf16[56,576]{1,0:T(8,128)(2,1)S(1)} %shard_map.44), channel_id=2, replica_groups=mesh['x'=4,'core'=2,'block'=4,'near'=8,'y'=4] {'x','core'}, dimensions={0}, use_global_device_ids=true | all-gather | bytes 580608 | tf_op jit(solution)/shard_map/all_gather | solution.py:208
  146.7 0.8 copy.5
  (1 shorter events, 0.0 us)
Async XLA Ops:
  0.6 28.0 %copy-start = (f32[1,56,576]{2,1,0:T(8,128)S(1)}, f32[1,56,576]{2,1,0:T(8,128)}, u32[]{:S(2)}) copy-start(f32[1,56,576]{2,1,0:T(8,128)} %param.3) | copy-start | bytes 387076

commit v5 on v4

--- a/solution.py
+++ b/solution.py
@@ -119,26 +119,29 @@
     def dot(a, b):
         return jnp.dot(a, b, preferred_element_type=jnp.float32)
 
+    columns = [slice(start, min(start + 2 * TILE, WIDE)) for start in range(0, WIDE, 2 * TILE)]
+    rows = rows_ref[...]
     g = gram[...]
-    square = dot(g, g) * inv_square
-    poly[...] = (
-        (cubic_coeff * g.astype(jnp.float32) + quintic_coeff * square) * inv_square
-    ).astype(poly.dtype)
-    half = (linear_coeff * g.astype(jnp.float32) + dot(g, poly[...])) * inv_square
-    work[...] = half.astype(work.dtype)
-    second = (linear_coeff * half + dot(poly[...], work[...])).astype(gram.dtype)
-
-    rows = rows_ref[...]
-    first = (linear_coeff * rows.astype(jnp.float32) + dot(rows, poly[...])) * inv_norm
-    first = first.astype(jnp.bfloat16)
-
-    gram[...] = second
+    for at in columns:
+        scaled = (cubic_coeff * inv_square) * gram[:, at].astype(jnp.float32)
+        square = (quintic_coeff * inv_square * inv_square) * dot(g, gram[:, at])
+        poly[:, at] = (scaled + square).astype(poly.dtype)
+    p = poly[...]
+    for at in columns:
+        scaled = (linear_coeff * inv_square) * gram[:, at].astype(jnp.float32)
+        work[:, at] = (scaled + inv_square * dot(g, poly[:, at])).astype(work.dtype)
+    first = ((linear_coeff * inv_norm) * rows.astype(jnp.float32) + inv_norm * dot(rows, p)).astype(
+        jnp.bfloat16
+    )
+    for at in columns:
+        half = linear_coeff * work[:, at].astype(jnp.float32)
+        gram[:, at] = (half + dot(p, work[:, at])).astype(gram.dtype)
     g = gram[...]
-    work[...] = (
-        cubic_coeff * g.astype(jnp.float32) + quintic_coeff * dot(g, g)
-    ).astype(work.dtype)
-    result = linear_coeff * first.astype(jnp.float32) + dot(first, work[...])
-    out_ref[...] = (result * factor)[:, : out_ref.shape[1]].astype(out_ref.dtype)
+    for at in columns:
+        scaled = cubic_coeff * gram[:, at].astype(jnp.float32)
+        work[:, at] = (scaled + quintic_coeff * dot(g, gram[:, at])).astype(work.dtype)
+    result = (linear_coeff * factor) * first.astype(jnp.float32) + factor * dot(first, work[...])
+    out_ref[...] = result[:, : out_ref.shape[1]].astype(out_ref.dtype)
 
 
 VMEM = pl.BlockSpec(memory_space=pltpu.VMEM)
@@ -190,17 +193,18 @@
 
 def local(partial_grads, momentum):
     rep, cluster = ("x", "core"), ("near", "y")
-    blocks = lax.axis_size("block")
+    pair, quads = lax.axis_size("pair"), lax.axis_size("quad")
     members = lax.axis_size(cluster)
     row_count, kv_width = momentum.shape[1:]
-    factor = 0.2 * math.sqrt(max(row_count * blocks * members, kv_width))
+    factor = 0.2 * math.sqrt(max(row_count * pair * quads * members, kv_width))
 
     received = lax.all_to_all(partial_grads[0], rep, 0, 0, tiled=True)
     wide, packed, new_momentum = gram(received, momentum[0])
 
     packed = packed.reshape(members, GROUPS * PACKED // members, TILE)
     packed = lax.all_to_all(packed, cluster, 0, 0, tiled=True)
-    packed = lax.all_to_all(total_of(packed, blocks), "block", 0, 0, tiled=True)
+    packed = lax.all_to_all(total_of(packed, pair), "pair", 0, 0, tiled=True)
+    packed = lax.all_to_all(total_of(packed, quads), "quad", 0, 0, tiled=True)
     packed = lax.all_to_all(total_of(packed, members), cluster, 0, 0, tiled=True)
     packed = packed.reshape(GROUPS * PACKED, TILE)
 
@@ -211,8 +215,8 @@
 
 def solution(mesh):
     devices = np.asarray(mesh.devices)
-    fine = Mesh(devices.reshape(4, 2, 4, 8, 4), ("x", "core", "block", "near", "y"))
-    rep, shard = ("x", "core"), ("block", "near", "y")
+    fine = Mesh(devices.reshape(4, 2, 4, 2, 4, 4), ("x", "core", "quad", "pair", "near", "y"))
+    rep, shard = ("x", "core"), ("quad", "pair", "near", "y")
     return jax.shard_map(
         local,
         mesh=fine,

time: 148 us -> 134 us (0.905)
  blocking collectives: 141 us -> 128 us
    all_to_all x1, blocking collectives: 29.4 us -> 14.2 us  [local(): lax.all_to_all(total_of(packed, members), cluster, 0, 0, tiled=True)]
    all_to_all x1, blocking collectives: 23.4 us -> 14.5 us  [local(): packed = lax.all_to_all(packed, cluster, 0, 0, tiled=True)]
    all_to_all x1 -> x2, blocking collectives: 42.2 us -> 50.9 us  [the longest x1 41.7 us: local(): packed = lax.all_to_all(total_of(packed, quads), 'quad', 0, 0, tiled=True)]
    all_gather x1, blocking collectives: 18.3 us -> 20.4 us  [local(): update = lax.all_gather(update, rep, axis=0, tiled=False)]
where the time goes in v5:
time: 134 us
  blocking collectives  128 us (96%)
  Pallas kernels  4.61 us (3%)
    all_to_all x1, blocking collectives, local(): packed = lax.all_to_all(total_of(packed, quads), 'quad', 0, 0, tiled=True)  41.7 us
    all_to_all x1, blocking collectives, local(): received = lax.all_to_all(partial_grads[0], rep, 0, 0, tiled=True)  28 us
    all_gather x1, blocking collectives, local(): update = lax.all_gather(update, rep, axis=0, tiled=False)  20.4 us
    all_to_all x1, blocking collectives, local(): packed = lax.all_to_all(packed, cluster, 0, 0, tiled=True)  14.5 us
    all_to_all x1, blocking collectives, local(): lax.all_to_all(total_of(packed, members), cluster, 0, 0, tiled=True)  14.2 us
    all_to_all x1, blocking collectives, local(): packed = lax.all_to_all(total_of(packed, pair), 'pair', 0, 0, tiled=True)  9.16 us
    pallas_call x1, Pallas kernels, newton(): pl.pallas_call(functools.partial(newton_kernel, factor), out_shape=bf16(w...  3.56 us

profile of v5, /device:TPU:1, one launch (start us, length us, event | category | flops | bytes accessed | tf_op | source)
XLA Modules:
  0.0 134.1 jit_solution(775999666055799438)
XLA Ops:
  0.6 0.0 copy-start
  0.6 28.0 %all_to_all.25.received_ref = bf16[8,56,576]{2,1,0:T(8,128)(2,1)S(1)} all-to-all(bf16[8,56,576]{2,1,0:T(8,128)(2,1)} %bitcast.10), channel_id=1, replica_groups=mesh['x'=4,'core'=2,'quad'=4,'pair'=2,'near'=4,'y'=4] {'x','core'}, dimensions={0} | all-to-all | bytes 1032192 | tf_op jit(solution)/shard_map/all_to_all | solution.py:201
  28.6 0.0 copy-done
  28.6 0.9 shard_map.41
  29.6 14.5 %all_to_all.26.parts_ref = bf16[16,96,128]{2,1,0:T(8,128)(2,1)S(1)} all-to-all(bf16[16,96,128]{2,1,0:T(8,128)(2,1)S(1)} %bitcast.7), channel_id=1, replica_groups=mesh['x'=4,'core'=2,'quad'=4,'pair'=2,'near'=4,'y'=4] {'near','y'}, dimensions={0} | all-to-all | bytes 786432 | tf_op jit(solution)/shard_map/all_to_all | solution.py:205
  44.1 0.1 shard_map.42
  44.2 9.2 %all_to_all.27.parts_ref = bf16[2,96,128]{2,1,0:T(8,128)(2,1)S(1)} all-to-all(bf16[2,96,128]{2,1,0:T(8,128)(2,1)S(1)} %shard_map.42), channel_id=1, replica_groups=mesh['x'=4,'core'=2,'quad'=4,'pair'=2,'near'=4,'y'=4] {'pair'}, dimensions={0} | all-to-all | bytes 98304 | tf_op jit(solution)/shard_map/all_to_all | solution.py:206
  53.3 41.7 %all_to_all.28.parts_ref = bf16[4,96,128]{2,1,0:T(8,128)(2,1)S(1)} all-to-all(bf16[4,96,128]{2,1,0:T(8,128)(2,1)S(1)} %shard_map.43), channel_id=1, replica_groups=mesh['x'=4,'core'=2,'quad'=4,'pair'=2,'near'=4,'y'=4] {'quad'}, dimensions={0} | all-to-all | bytes 196608 | tf_op jit(solution)/shard_map/all_to_all | solution.py:207
  95.1 14.2 %all_to_all.29 = bf16[16,96,128]{2,1,0:T(8,128)(2,1)S(1)} all-to-all(bf16[16,96,128]{2,1,0:T(8,128)(2,1)S(1)} %shard_map.44), channel_id=1, replica_groups=mesh['x'=4,'core'=2,'quad'=4,'pair'=2,'near'=4,'y'=4] {'near','y'}, dimensions={0} | all-to-all | bytes 786432 | tf_op jit(solution)/shard_map/all_to_all | solution.py:208
  109.3 3.6 %shard_map.45 = bf16[56,576]{1,0:T(8,128)(2,1)S(1)} custom-call(bf16[1536,128]{1,0:T(8,128)(2,1)S(1)} %bitcast.6, bf16[56,640]{1,0:T(8,128)(2,1)S(1)} %get-tuple-element.6.rows_ref), custom_call_target="tpu_custom_call" | custom-call | tf_op jit(solution)/shard_map/pallas_call | solution.py:184
  112.9 20.4 %all-gather = bf16[448,576]{1,0:T(8,128)(2,1)S(1)} all-gather(bf16[56,576]{1,0:T(8,128)(2,1)S(1)} %shard_map.45), channel_id=2, replica_groups=mesh['x'=4,'core'=2,'quad'=4,'pair'=2,'near'=4,'y'=4] {'x','core'}, dimensions={0}, use_global_device_ids=true | all-gather | bytes 580608 | tf_op jit(solution)/shard_map/all_gather | solution.py:212
  133.3 0.8 copy.5
  (2 shorter events, 0.0 us)
Async XLA Ops:
  0.6 28.0 %copy-start = (f32[1,56,576]{2,1,0:T(8,128)S(1)}, f32[1,56,576]{2,1,0:T(8,128)}, u32[]{:S(2)}) copy-start(f32[1,56,576]{2,1,0:T(8,128)} %param.3) | copy-start | bytes 387076

commit v6 on v5

--- a/solution.py
+++ b/solution.py
@@ -119,29 +119,45 @@
     def dot(a, b):
         return jnp.dot(a, b, preferred_element_type=jnp.float32)
 
-    columns = [slice(start, min(start + 2 * TILE, WIDE)) for start in range(0, WIDE, 2 * TILE)]
+    edges = [(0, 2 * TILE), (2 * TILE, 4 * TILE), (4 * TILE, WIDE)]
+
+    def symmetric(store, product):
+        for start, stop in edges:
+            to = min(stop, WIDE - HALF)
+            block = product(slice(0, to), slice(start, stop))
+            store[0:to, start:stop] = block.astype(store.dtype)
+            if start:
+                store[start:stop, 0:start] = block[:start].T.astype(store.dtype)
+
     rows = rows_ref[...]
-    g = gram[...]
-    for at in columns:
-        scaled = (cubic_coeff * inv_square) * gram[:, at].astype(jnp.float32)
-        square = (quintic_coeff * inv_square * inv_square) * dot(g, gram[:, at])
-        poly[:, at] = (scaled + square).astype(poly.dtype)
-    p = poly[...]
-    for at in columns:
-        scaled = (linear_coeff * inv_square) * gram[:, at].astype(jnp.float32)
-        work[:, at] = (scaled + inv_square * dot(g, poly[:, at])).astype(work.dtype)
-    first = ((linear_coeff * inv_norm) * rows.astype(jnp.float32) + inv_norm * dot(rows, p)).astype(
-        jnp.bfloat16
-    )
-    for at in columns:
-        half = linear_coeff * work[:, at].astype(jnp.float32)
-        gram[:, at] = (half + dot(p, work[:, at])).astype(gram.dtype)
-    g = gram[...]
-    for at in columns:
-        scaled = cubic_coeff * gram[:, at].astype(jnp.float32)
-        work[:, at] = (scaled + quintic_coeff * dot(g, gram[:, at])).astype(work.dtype)
+    for store in (poly, work):
+        store[WIDE - HALF :, WIDE - TILE :] = jnp.zeros((HALF, TILE), store.dtype)
+    symmetric(
+        poly,
+        lambda to, at: (cubic_coeff * inv_square) * gram[to, at].astype(jnp.float32)
+        + (quintic_coeff * inv_square * inv_square) * dot(gram[to, :], gram[:, at]),
+    )
+    symmetric(
+        work,
+        lambda to, at: (linear_coeff * inv_square) * gram[to, at].astype(jnp.float32)
+        + inv_square * dot(gram[to, :], poly[:, at]),
+    )
+    first = (linear_coeff * inv_norm) * rows.astype(jnp.float32) + inv_norm * dot(rows, poly[...])
+    first = first.astype(jnp.bfloat16)
+    symmetric(
+        gram,
+        lambda to, at: linear_coeff * work[to, at].astype(jnp.float32)
+        + dot(poly[to, :], work[:, at]),
+    )
+    symmetric(
+        work,
+        lambda to, at: cubic_coeff * gram[to, at].astype(jnp.float32)
+        + quintic_coeff * dot(gram[to, :], gram[:, at]),
+    )
     result = (linear_coeff * factor) * first.astype(jnp.float32) + factor * dot(first, work[...])
-    out_ref[...] = result[:, : out_ref.shape[1]].astype(out_ref.dtype)
+    update = result[:, : out_ref.shape[2]].astype(out_ref.dtype)
+    for receiver in range(out_ref.shape[0]):
+        out_ref[receiver] = update
 
 
 VMEM = pl.BlockSpec(memory_space=pltpu.VMEM)
@@ -180,10 +196,10 @@
     )(parts)
 
 
-def newton(factor, packed, wide, width):
+def newton(factor, packed, wide, width, receivers):
     return pl.pallas_call(
         functools.partial(newton_kernel, factor),
-        out_shape=bf16(wide.shape[0], width),
+        out_shape=bf16(receivers, wide.shape[0], width),
         in_specs=[VMEM, VMEM],
         out_specs=VMEM,
         scratch_shapes=[pltpu.VMEM((WIDE, WIDE), jnp.bfloat16)] * 3,
@@ -208,9 +224,10 @@
     packed = lax.all_to_all(total_of(packed, members), cluster, 0, 0, tiled=True)
     packed = packed.reshape(GROUPS * PACKED, TILE)
 
-    update = newton(factor, packed, wide, kv_width)
-    update = lax.all_gather(update, rep, axis=0, tiled=False)
-    return (update, new_momentum[None])
+    update = newton(factor, packed, wide, kv_width, lax.axis_size("x"))
+    update = lax.all_to_all(update, "x", 0, 0, tiled=True)
+    update = lax.all_gather(update, "core", axis=1)
+    return (update.reshape(-1, row_count, kv_width), new_momentum[None])
 
 
 def solution(mesh):

time: 134 us -> 132 us (0.985)
  blocking collectives: 128 us -> 126 us
    all_gather x1, blocking collectives: 20.4 us -> 10.4 us  [local(): update = lax.all_gather(update, 'core', axis=1)]
    all_to_all x0 -> x1, blocking collectives: none -> 8.02 us  [local(): update = lax.all_to_all(update, 'x', 0, 0, tiled=True)]
where the time goes in v6:
time: 132 us; the launch traced here: 131 us
  blocking collectives  126 us (95%)
  Pallas kernels  3.79 us (3%)
    all_to_all x1, blocking collectives, local(): packed = lax.all_to_all(total_of(packed, quads), 'quad', 0, 0, tiled=True)  41.7 us
    all_to_all x1, blocking collectives, local(): received = lax.all_to_all(partial_grads[0], rep, 0, 0, tiled=True)  28 us
    all_to_all x1, blocking collectives, local(): packed = lax.all_to_all(packed, cluster, 0, 0, tiled=True)  14.5 us
    all_to_all x1, blocking collectives, local(): lax.all_to_all(total_of(packed, members), cluster, 0, 0, tiled=True)  14.2 us
    all_gather x1, blocking collectives, local(): update = lax.all_gather(update, 'core', axis=1)  10.4 us
    all_to_all x1, blocking collectives, local(): packed = lax.all_to_all(total_of(packed, pair), 'pair', 0, 0, tiled=True)  9.16 us
    all_to_all x1, blocking collectives, local(): update = lax.all_to_all(update, 'x', 0, 0, tiled=True)  8.02 us
    pallas_call x1, Pallas kernels, newton(): pl.pallas_call(functools.partial(newton_kernel, factor), out_shape=bf16(r...  2.74 us

profile of v6, /device:TPU:1, one launch (start us, length us, event | category | flops | bytes accessed | tf_op | source)
XLA Modules:
  0.0 131.3 jit_solution(11905031291126098355)
XLA Ops:
  0.6 0.0 copy-start
  0.6 28.0 %all_to_all.30.received_ref = bf16[8,56,576]{2,1,0:T(8,128)(2,1)S(1)} all-to-all(bf16[8,56,576]{2,1,0:T(8,128)(2,1)} %bitcast.10), channel_id=1, replica_groups=mesh['x'=4,'core'=2,'quad'=4,'pair'=2,'near'=4,'y'=4] {'x','core'}, dimensions={0} | all-to-all | bytes 1032192 | tf_op jit(solution)/shard_map/all_to_all | solution.py:217
  28.6 0.0 copy-done
  28.6 0.9 shard_map.41
  29.6 14.5 %all_to_all.31.parts_ref = bf16[16,96,128]{2,1,0:T(8,128)(2,1)S(1)} all-to-all(bf16[16,96,128]{2,1,0:T(8,128)(2,1)S(1)} %bitcast.7), channel_id=1, replica_groups=mesh['x'=4,'core'=2,'quad'=4,'pair'=2,'near'=4,'y'=4] {'near','y'}, dimensions={0} | all-to-all | bytes 786432 | tf_op jit(solution)/shard_map/all_to_all | solution.py:221
  44.1 0.1 shard_map.42
  44.2 9.2 %all_to_all.32.parts_ref = bf16[2,96,128]{2,1,0:T(8,128)(2,1)S(1)} all-to-all(bf16[2,96,128]{2,1,0:T(8,128)(2,1)S(1)} %shard_map.42), channel_id=1, replica_groups=mesh['x'=4,'core'=2,'quad'=4,'pair'=2,'near'=4,'y'=4] {'pair'}, dimensions={0} | all-to-all | bytes 98304 | tf_op jit(solution)/shard_map/all_to_all | solution.py:222
  53.3 41.7 %all_to_all.33.parts_ref = bf16[4,96,128]{2,1,0:T(8,128)(2,1)S(1)} all-to-all(bf16[4,96,128]{2,1,0:T(8,128)(2,1)S(1)} %shard_map.43), channel_id=1, replica_groups=mesh['x'=4,'core'=2,'quad'=4,'pair'=2,'near'=4,'y'=4] {'quad'}, dimensions={0} | all-to-all | bytes 196608 | tf_op jit(solution)/shard_map/all_to_all | solution.py:223
  95.1 14.2 %all_to_all.34 = bf16[16,96,128]{2,1,0:T(8,128)(2,1)S(1)} all-to-all(bf16[16,96,128]{2,1,0:T(8,128)(2,1)S(1)} %shard_map.44), channel_id=1, replica_groups=mesh['x'=4,'core'=2,'quad'=4,'pair'=2,'near'=4,'y'=4] {'near','y'}, dimensions={0} | all-to-all | bytes 786432 | tf_op jit(solution)/shard_map/all_to_all | solution.py:224
  109.3 2.7 %shard_map.45 = bf16[4,56,576]{2,1,0:T(8,128)(2,1)S(1)} custom-call(bf16[1536,128]{1,0:T(8,128)(2,1)S(1)} %bitcast.6, bf16[56,640]{1,0:T(8,128)(2,1)S(1)} %get-tuple-element.6.rows_ref), custom_call_target="tpu_custom_call" | custom-call | tf_op jit(solution)/shard_map/pallas_call | solution.py:200
  112.1 8.0 %all_to_all.35 = bf16[4,56,576]{2,1,0:T(8,128)(2,1)S(1)} all-to-all(bf16[4,56,576]{2,1,0:T(8,128)(2,1)S(1)} %shard_map.45), channel_id=1, replica_groups=mesh['x'=4,'core'=2,'quad'=4,'pair'=2,'near'=4,'y'=4] {'x'}, dimensions={0} | all-to-all | bytes 516096 | tf_op jit(solution)/shard_map/all_to_all | solution.py:228
  120.1 10.4 %all-gather = bf16[4,112,576]{2,1,0:T(8,128)(2,1)S(1)} all-gather(bf16[4,56,576]{2,1,0:T(8,128)(2,1)S(1)} %all_to_all.35), channel_id=2, replica_groups=mesh['x'=4,'core'=2,'quad'=4,'pair'=2,'near'=4,'y'=4] {'core'}, dimensions={1}, use_global_device_ids=true | all-gather | bytes 774144 | tf_op jit(solution)/shard_map/all_gather | solution.py:229
  130.5 0.8 copy.5
  (2 shorter events, 0.0 us)
Async XLA Ops:
  0.6 28.0 %copy-start = (f32[1,56,576]{2,1,0:T(8,128)S(1)}, f32[1,56,576]{2,1,0:T(8,128)}, u32[]{:S(2)}) copy-start(f32[1,56,576]{2,1,0:T(8,128)} %param.3) | copy-start | bytes 387076

commit v7 on v6

--- a/solution.py
+++ b/solution.py
@@ -209,18 +209,17 @@
 
 def local(partial_grads, momentum):
     rep, cluster = ("x", "core"), ("near", "y")
-    pair, quads = lax.axis_size("pair"), lax.axis_size("quad")
+    blocks = lax.axis_size("block")
     members = lax.axis_size(cluster)
     row_count, kv_width = momentum.shape[1:]
-    factor = 0.2 * math.sqrt(max(row_count * pair * quads * members, kv_width))
+    factor = 0.2 * math.sqrt(max(row_count * blocks * members, kv_width))
 
     received = lax.all_to_all(partial_grads[0], rep, 0, 0, tiled=True)
     wide, packed, new_momentum = gram(received, momentum[0])
 
     packed = packed.reshape(members, GROUPS * PACKED // members, TILE)
     packed = lax.all_to_all(packed, cluster, 0, 0, tiled=True)
-    packed = lax.all_to_all(total_of(packed, pair), "pair", 0, 0, tiled=True)
-    packed = lax.all_to_all(total_of(packed, quads), "quad", 0, 0, tiled=True)
+    packed = lax.all_to_all(total_of(packed, blocks), "block", 0, 0, tiled=True)
     packed = lax.all_to_all(total_of(packed, members), cluster, 0, 0, tiled=True)
     packed = packed.reshape(GROUPS * PACKED, TILE)
 
@@ -232,8 +231,8 @@
 
 def solution(mesh):
     devices = np.asarray(mesh.devices)
-    fine = Mesh(devices.reshape(4, 2, 4, 2, 4, 4), ("x", "core", "quad", "pair", "near", "y"))
-    rep, shard = ("x", "core"), ("quad", "pair", "near", "y")
+    fine = Mesh(devices.reshape(4, 2, 8, 4, 4), ("x", "core", "block", "near", "y"))
+    rep, shard = ("x", "core"), ("block", "near", "y")
     return jax.shard_map(
         local,
         mesh=fine,

time: 132 us -> 130 us (0.985)
  blocking collectives: 126 us -> 124 us
    all_to_all x1, blocking collectives: 14.2 us -> 18.1 us  [local(): lax.all_to_all(total_of(packed, members), cluster, 0, 0, tiled=True)]
    all_gather x1, blocking collectives: 10.4 us -> 7.1 us  [local(): update = lax.all_gather(update, 'core', axis=1)]
    all_to_all x2 -> x1, blocking collectives: 50.9 us -> 48.1 us  [local(): packed = lax.all_to_all(total_of(packed, blocks), 'block', 0, 0, tiled=True)]
where the time goes in v7:
time: 130 us; the launch traced here: 129 us
  blocking collectives  124 us (95%)
  Pallas kernels  3.78 us (3%)
    all_to_all x1, blocking collectives, local(): packed = lax.all_to_all(total_of(packed, blocks), 'block', 0, 0, tiled=True)  48.1 us
    all_to_all x1, blocking collectives, local(): received = lax.all_to_all(partial_grads[0], rep, 0, 0, tiled=True)  28 us
    all_to_all x1, blocking collectives, local(): lax.all_to_all(total_of(packed, members), cluster, 0, 0, tiled=True)  18.1 us
    all_to_all x1, blocking collectives, local(): packed = lax.all_to_all(packed, cluster, 0, 0, tiled=True)  14.5 us
    all_to_all x1, blocking collectives, local(): update = lax.all_to_all(update, 'x', 0, 0, tiled=True)  8.02 us
    all_gather x1, blocking collectives, local(): update = lax.all_gather(update, 'core', axis=1)  7.1 us
    pallas_call x1, Pallas kernels, newton(): pl.pallas_call(functools.partial(newton_kernel, factor), out_shape=bf16(r...  2.74 us

profile of v7, /device:TPU:1, one launch (start us, length us, event | category | flops | bytes accessed | tf_op | source)
XLA Modules:
  0.0 129.2 jit_solution(13371705428626108898)
XLA Ops:
  0.6 0.0 copy-start
  0.6 28.0 %all_to_all.25.received_ref = bf16[8,56,576]{2,1,0:T(8,128)(2,1)S(1)} all-to-all(bf16[8,56,576]{2,1,0:T(8,128)(2,1)} %bitcast.10), channel_id=1, replica_groups=mesh['x'=4,'core'=2,'block'=8,'near'=4,'y'=4] {'x','core'}, dimensions={0} | all-to-all | bytes 1032192 | tf_op jit(solution)/shard_map/all_to_all | solution.py:217
  28.6 0.0 copy-done
  28.6 0.9 shard_map.41
  29.6 14.5 %all_to_all.26.parts_ref = bf16[16,96,128]{2,1,0:T(8,128)(2,1)S(1)} all-to-all(bf16[16,96,128]{2,1,0:T(8,128)(2,1)S(1)} %bitcast.7), channel_id=1, replica_groups=mesh['x'=4,'core'=2,'block'=8,'near'=4,'y'=4] {'near','y'}, dimensions={0} | all-to-all | bytes 786432 | tf_op jit(solution)/shard_map/all_to_all | solution.py:221
  44.1 0.1 shard_map.42
  44.2 48.1 %all_to_all.27.parts_ref = bf16[8,96,128]{2,1,0:T(8,128)(2,1)S(1)} all-to-all(bf16[8,96,128]{2,1,0:T(8,128)(2,1)S(1)} %shard_map.42), channel_id=1, replica_groups=mesh['x'=4,'core'=2,'block'=8,'near'=4,'y'=4] {'block'}, dimensions={0} | all-to-all | bytes 393216 | tf_op jit(solution)/shard_map/all_to_all | solution.py:222
  92.3 18.1 %all_to_all.28 = bf16[16,96,128]{2,1,0:T(8,128)(2,1)S(1)} all-to-all(bf16[16,96,128]{2,1,0:T(8,128)(2,1)S(1)} %shard_map.43), channel_id=1, replica_groups=mesh['x'=4,'core'=2,'block'=8,'near'=4,'y'=4] {'near','y'}, dimensions={0} | all-to-all | bytes 786432 | tf_op jit(solution)/shard_map/all_to_all | solution.py:223
  110.5 2.7 %shard_map.44 = bf16[4,56,576]{2,1,0:T(8,128)(2,1)S(1)} custom-call(bf16[1536,128]{1,0:T(8,128)(2,1)S(1)} %bitcast.6, bf16[56,640]{1,0:T(8,128)(2,1)S(1)} %get-tuple-element.6.rows_ref), custom_call_target="tpu_custom_call" | custom-call | tf_op jit(solution)/shard_map/pallas_call | solution.py:200
  113.2 8.0 %all_to_all.29 = bf16[4,56,576]{2,1,0:T(8,128)(2,1)S(1)} all-to-all(bf16[4,56,576]{2,1,0:T(8,128)(2,1)S(1)} %shard_map.44), channel_id=1, replica_groups=mesh['x'=4,'core'=2,'block'=8,'near'=4,'y'=4] {'x'}, dimensions={0} | all-to-all | bytes 516096 | tf_op jit(solution)/shard_map/all_to_all | solution.py:227
  121.3 7.1 %all-gather = bf16[4,112,576]{2,1,0:T(8,128)(2,1)S(1)} all-gather(bf16[4,56,576]{2,1,0:T(8,128)(2,1)S(1)} %all_to_all.29), channel_id=2, replica_groups=mesh['x'=4,'core'=2,'block'=8,'near'=4,'y'=4] {'core'}, dimensions={1}, use_global_device_ids=true | all-gather | bytes 774144 | tf_op jit(solution)/shard_map/all_gather | solution.py:228
  128.4 0.8 copy.5
  (1 shorter events, 0.0 us)
Async XLA Ops:
  0.6 28.0 %copy-start = (f32[1,56,576]{2,1,0:T(8,128)S(1)}, f32[1,56,576]{2,1,0:T(8,128)}, u32[]{:S(2)}) copy-start(f32[1,56,576]{2,1,0:T(8,128)} %param.3) | copy-start | bytes 387076

commit v8 on v7

--- a/solution.py
+++ b/solution.py
@@ -21,11 +21,11 @@
 TILES = 5
 WIDE = TILE * TILES
 GROUPS = 4
-PACKED = 384
-
-
-def left_half(rows):
-    return lax.broadcasted_iota(jnp.int32, (rows, TILE), 1) < HALF
+ACROSS, BELOW, DIAGONAL, CORNER, PACKED = 512, 768, 1024, 1280, 1408
+
+
+def places(rows):
+    return (lax.broadcasted_iota(jnp.int32, (rows, TILE), axis) for axis in range(2))
 
 
 def gram_kernel(
@@ -57,18 +57,21 @@
     def put(start, block):
         packed_ref[start : start + block.shape[0], :] = block.astype(packed_ref.dtype)
 
-    last = tile(4, 4)[:HALF]
+    row, col = places(HALF)
+    corner = tile(4, 4)[:HALF]
     for y in range(GROUPS):
-        base = y * PACKED
-        put(base, tile(y, (y + 1) % 4))
-        put(base + 192, tile(4, y)[:HALF])
-        diagonal = tile(y, y)
-        put(base + 256, diagonal[:HALF])
-        put(base + 320, jnp.where(left_half(HALF), last, diagonal[HALF:]))
+        put(y * TILE, tile(y, (y + 1) % 4))
+        put(BELOW + y * HALF, tile(4, y)[:HALF])
+        square = tile(y, y)
+        upper, lower = square[:HALF], square[HALF:]
+        moved = jnp.concatenate([lower[:, HALF:], lower[:, :HALF]], axis=1)
+        put(DIAGONAL + y * HALF, jnp.where(row > col, moved, upper))
+        line = jnp.sum(jnp.where(row == col, moved, 0.0), axis=1, keepdims=True)
+        corner = jnp.where(col == HALF + y, line, corner)
     for i in range(2):
-        split = tile(i, i + 2)
-        put(i * PACKED + 128, split[:HALF])
-        put((i + 2) * PACKED + 128, split[HALF:])
+        put(ACROSS + i * TILE, tile(i, i + 2))
+    put(CORNER, corner)
+    put(CORNER + HALF, jnp.zeros((HALF, TILE), jnp.float32))
     write.wait()
 
 
@@ -83,12 +86,10 @@
 
 def newton_kernel(factor, packed_ref, rows_ref, out_ref, gram, work, poly):
     zeros = jnp.zeros((HALF, TILE), jnp.float32)
-    row = lax.broadcasted_iota(jnp.int32, (HALF, TILE), 0)
-    col = lax.broadcasted_iota(jnp.int32, (HALF, TILE), 1)
-    trace = zeros
-
-    def part(y, start, stop):
-        return packed_ref[y * PACKED + start : y * PACKED + stop, :].astype(jnp.float32)
+    row, col = places(HALF)
+
+    def part(start, rows):
+        return packed_ref[start : start + rows, :].astype(jnp.float32)
 
     def put(i, j, tile):
         gram[i * TILE : (i + 1) * TILE, j * TILE : (j + 1) * TILE] = tile.astype(gram.dtype)
@@ -97,20 +98,24 @@
         put(i, j, tile)
         put(j, i, tile.T)
 
+    corner = part(CORNER, HALF)
+    block = jnp.where(col < HALF, corner, 0.0)
+    put(4, 4, jnp.concatenate([block, zeros], axis=0))
+    trace = jnp.where(row == col, block, 0.0)
     for y in range(GROUPS):
-        put_both(y, (y + 1) % 4, part(y, 0, 128))
-        put_both(4, y, jnp.concatenate([part(y, 192, 256), zeros], axis=0))
-        upper, corner = part(y, 256, 320), part(y, 320, 384)
-        mirrored = jnp.concatenate([upper, zeros], axis=0).T
-        lower = jnp.where(left_half(HALF), mirrored[HALF:], corner)
+        put_both(y, (y + 1) % 4, part(y * TILE, TILE))
+        put_both(4, y, jnp.concatenate([part(BELOW + y * HALF, HALF), zeros], axis=0))
+        square = part(DIAGONAL + y * HALF, HALF)
+        turned = jnp.concatenate([square, zeros], axis=0).T
+        line = jnp.where(col == HALF + y, corner, 0.0)
+        trace += jnp.where(row == col, square, 0.0) + line
+        line = jnp.sum(line, axis=1, keepdims=True)
+        upper = jnp.where(row > col, turned[:HALF], square)
+        lower = jnp.where(row > col, square, jnp.where(row < col, turned[:HALF], line))
+        lower = jnp.concatenate([turned[HALF:, :HALF], lower[:, :HALF]], axis=1)
         put(y, y, jnp.concatenate([upper, lower], axis=0))
-        trace += jnp.where(row == col, upper, 0.0) + jnp.where(row + HALF == col, corner, 0.0)
-        if y == 0:
-            trace += jnp.where(row == col, corner, 0.0)
-            last = jnp.where(left_half(HALF), corner, 0.0)
-            put(4, 4, jnp.concatenate([last, zeros], axis=0))
     for i in range(2):
-        put_both(i, i + 2, jnp.concatenate([part(i, 128, 192), part(i + 2, 128, 192)], axis=0))
+        put_both(i, i + 2, part(ACROSS + i * TILE, TILE))
 
     total = jnp.sum(trace, axis=(0, 1), keepdims=True)
     inv_norm = 1.0 / (jnp.sqrt(total) + norm_eps)
@@ -175,7 +180,7 @@
         gram_kernel,
         out_shape=(
             bf16(rows, WIDE),
-            bf16(GROUPS * PACKED, TILE),
+            bf16(PACKED, TILE),
             jax.ShapeDtypeStruct(momentum.shape, momentum.dtype),
         ),
         in_specs=[VMEM, HBM],
@@ -217,11 +222,11 @@
     received = lax.all_to_all(partial_grads[0], rep, 0, 0, tiled=True)
     wide, packed, new_momentum = gram(received, momentum[0])
 
-    packed = packed.reshape(members, GROUPS * PACKED // members, TILE)
+    packed = packed.reshape(members, PACKED // members, TILE)
     packed = lax.all_to_all(packed, cluster, 0, 0, tiled=True)
     packed = lax.all_to_all(total_of(packed, blocks), "block", 0, 0, tiled=True)
     packed = lax.all_to_all(total_of(packed, members), cluster, 0, 0, tiled=True)
-    packed = packed.reshape(GROUPS * PACKED, TILE)
+    packed = packed.reshape(PACKED, TILE)
 
     update = newton(factor, packed, wide, kv_width, lax.axis_size("x"))
     update = lax.all_to_all(update, "x", 0, 0, tiled=True)

time: 130 us -> 126 us (0.969)
  blocking collectives: 124 us -> 120 us
    all_to_all x1, blocking collectives: 48.1 us -> 45.4 us  [local(): packed = lax.all_to_all(total_of(packed, blocks), 'block', 0, 0, tiled=True)]
where the time goes in v8:
time: 126 us
  blocking collectives  120 us (95%)
  Pallas kernels  4.03 us (3%)
    all_to_all x1, blocking collectives, local(): packed = lax.all_to_all(total_of(packed, blocks), 'block', 0, 0, tiled=True)  45.4 us
    all_to_all x1, blocking collectives, local(): received = lax.all_to_all(partial_grads[0], rep, 0, 0, tiled=True)  28 us
    all_to_all x1, blocking collectives, local(): lax.all_to_all(total_of(packed, members), cluster, 0, 0, tiled=True)  17.4 us
    all_to_all x1, blocking collectives, local(): packed = lax.all_to_all(packed, cluster, 0, 0, tiled=True)  14 us
    all_to_all x1, blocking collectives, local(): update = lax.all_to_all(update, 'x', 0, 0, tiled=True)  8.56 us
    all_gather x1, blocking collectives, local(): update = lax.all_gather(update, 'core', axis=1)  7.02 us
    pallas_call x1, Pallas kernels, newton(): pl.pallas_call(functools.partial(newton_kernel, factor), out_shape=bf16(r...  2.99 us

profile of v8, /device:TPU:1, one launch (start us, length us, event | category | flops | bytes accessed | tf_op | source)
XLA Modules:
  0.0 125.9 jit_solution(13392571170744044054)
XLA Ops:
  0.6 0.0 copy-start
  0.6 28.0 %all_to_all.25.received_ref = bf16[8,56,576]{2,1,0:T(8,128)(2,1)S(1)} all-to-all(bf16[8,56,576]{2,1,0:T(8,128)(2,1)} %bitcast.10), channel_id=1, replica_groups=mesh['x'=4,'core'=2,'block'=8,'near'=4,'y'=4] {'x','core'}, dimensions={0} | all-to-all | bytes 1032192 | tf_op jit(solution)/shard_map/all_to_all | solution.py:222
  28.6 0.0 copy-done
  28.6 0.9 shard_map.41
  29.6 14.0 %all_to_all.26.parts_ref = bf16[16,88,128]{2,1,0:T(8,128)(2,1)S(1)} all-to-all(bf16[16,88,128]{2,1,0:T(8,128)(2,1)S(1)} %bitcast.7), channel_id=1, replica_groups=mesh['x'=4,'core'=2,'block'=8,'near'=4,'y'=4] {'near','y'}, dimensions={0} | all-to-all | bytes 720896 | tf_op jit(solution)/shard_map/all_to_all | solution.py:226
  43.6 0.1 shard_map.42
  43.6 45.4 %all_to_all.27.parts_ref = bf16[8,88,128]{2,1,0:T(8,128)(2,1)S(1)} all-to-all(bf16[8,88,128]{2,1,0:T(8,128)(2,1)S(1)} %shard_map.42), channel_id=1, replica_groups=mesh['x'=4,'core'=2,'block'=8,'near'=4,'y'=4] {'block'}, dimensions={0} | all-to-all | bytes 360448 | tf_op jit(solution)/shard_map/all_to_all | solution.py:227
  89.1 17.4 %all_to_all.28 = bf16[16,88,128]{2,1,0:T(8,128)(2,1)S(1)} all-to-all(bf16[16,88,128]{2,1,0:T(8,128)(2,1)S(1)} %shard_map.43), channel_id=1, replica_groups=mesh['x'=4,'core'=2,'block'=8,'near'=4,'y'=4] {'near','y'}, dimensions={0} | all-to-all | bytes 720896 | tf_op jit(solution)/shard_map/all_to_all | solution.py:228
  106.5 3.0 %shard_map.44 = bf16[4,56,576]{2,1,0:T(8,128)(2,1)S(1)} custom-call(bf16[1408,128]{1,0:T(8,128)(2,1)S(1)} %bitcast.6, bf16[56,640]{1,0:T(8,128)(2,1)S(1)} %get-tuple-element.6.rows_ref), custom_call_target="tpu_custom_call" | custom-call | tf_op jit(solution)/shard_map/pallas_call | solution.py:205
  109.5 8.6 %all_to_all.29 = bf16[4,56,576]{2,1,0:T(8,128)(2,1)S(1)} all-to-all(bf16[4,56,576]{2,1,0:T(8,128)(2,1)S(1)} %shard_map.44), channel_id=1, replica_groups=mesh['x'=4,'core'=2,'block'=8,'near'=4,'y'=4] {'x'}, dimensions={0} | all-to-all | bytes 516096 | tf_op jit(solution)/shard_map/all_to_all | solution.py:232
  118.1 7.0 %all-gather = bf16[4,112,576]{2,1,0:T(8,128)(2,1)S(1)} all-gather(bf16[4,56,576]{2,1,0:T(8,128)(2,1)S(1)} %all_to_all.29), channel_id=2, replica_groups=mesh['x'=4,'core'=2,'block'=8,'near'=4,'y'=4] {'core'}, dimensions={1}, use_global_device_ids=true | all-gather | bytes 774144 | tf_op jit(solution)/shard_map/all_gather | solution.py:233
  125.1 0.8 copy.5
  (1 shorter events, 0.0 us)
Async XLA Ops:
  0.6 28.0 %copy-start = (f32[1,56,576]{2,1,0:T(8,128)S(1)}, f32[1,56,576]{2,1,0:T(8,128)}, u32[]{:S(2)}) copy-start(f32[1,56,576]{2,1,0:T(8,128)} %param.3) | copy-start | bytes 387076

commit v9 on v8

--- a/solution.py
+++ b/solution.py
@@ -96,7 +96,7 @@
 
     def put_both(i, j, tile):
         put(i, j, tile)
-        put(j, i, tile.T)
+        put(j, i, tile.astype(gram.dtype).T)
 
     corner = part(CORNER, HALF)
     block = jnp.where(col < HALF, corner, 0.0)
@@ -132,7 +132,7 @@
             block = product(slice(0, to), slice(start, stop))
             store[0:to, start:stop] = block.astype(store.dtype)
             if start:
-                store[start:stop, 0:start] = block[:start].T.astype(store.dtype)
+                store[start:stop, 0:start] = block[:start].astype(store.dtype).T
 
     rows = rows_ref[...]
     for store in (poly, work):
@@ -212,10 +212,17 @@
     )(packed, wide)
 
 
+def exchange(parts, axis, order):
+    return lax.all_to_all(parts, axis, 0, 0, axis_index_groups=[order], tiled=True)
+
+
 def local(partial_grads, momentum):
     rep, cluster = ("x", "core"), ("near", "y")
     blocks = lax.axis_size("block")
     members = lax.axis_size(cluster)
+    lanes = lax.axis_size("y")
+    cluster_order = [z * lanes + y for y in range(lanes) for z in range(members // lanes)]
+    block_order = [*range(0, blocks, 2), *range(1, blocks, 2)]
     row_count, kv_width = momentum.shape[1:]
     factor = 0.2 * math.sqrt(max(row_count * blocks * members, kv_width))
 
@@ -223,9 +230,9 @@
     wide, packed, new_momentum = gram(received, momentum[0])
 
     packed = packed.reshape(members, PACKED // members, TILE)
-    packed = lax.all_to_all(packed, cluster, 0, 0, tiled=True)
-    packed = lax.all_to_all(total_of(packed, blocks), "block", 0, 0, tiled=True)
-    packed = lax.all_to_all(total_of(packed, members), cluster, 0, 0, tiled=True)
+    packed = exchange(packed, cluster, cluster_order)
+    packed = exchange(total_of(packed, blocks), "block", block_order)
+    packed = exchange(total_of(packed, members), cluster, cluster_order)
     packed = packed.reshape(PACKED, TILE)
 
     update = newton(factor, packed, wide, kv_width, lax.axis_size("x"))

time: 126 us -> 125 us (level)
    all_to_all x3, blocking collectives: 76.8 us -> 72.3 us  [exchange(): lax.all_to_all(parts, axis, 0, 0, axis_index_groups=[order], tiled=True)]
    all_gather x1, blocking collectives: 7.02 us -> 10.5 us  [local(): update = lax.all_gather(update, 'core', axis=1)]
where the time goes in v9:
time: 125 us; the launch traced here: 124 us
  blocking collectives  119 us (95%)
  Pallas kernels  3.88 us (3%)
    all_to_all x3, blocking collectives, exchange(): lax.all_to_all(parts, axis, 0, 0, axis_index_groups=[order], tiled=True)  72.3 us
    all_to_all x1, blocking collectives, local(): received = lax.all_to_all(partial_grads[0], rep, 0, 0, tiled=True)  28 us
    all_gather x1, blocking collectives, local(): update = lax.all_gather(update, 'core', axis=1)  10.5 us
    all_to_all x1, blocking collectives, local(): update = lax.all_to_all(update, 'x', 0, 0, tiled=True)  8.02 us
    pallas_call x1, Pallas kernels, newton(): pl.pallas_call(functools.partial(newton_kernel, factor), out_shape=bf16(r...  2.83 us

profile of v9, /device:TPU:1, one launch (start us, length us, event | category | flops | bytes accessed | tf_op | source)
XLA Modules:
  0.0 124.2 jit_solution(13977235941721513291)
XLA Ops:
  0.6 0.0 copy-start
  0.6 28.0 %all_to_all.25.received_ref = bf16[8,56,576]{2,1,0:T(8,128)(2,1)S(1)} all-to-all(bf16[8,56,576]{2,1,0:T(8,128)(2,1)} %bitcast.10), channel_id=1, replica_groups=mesh['x'=4,'core'=2,'block'=8,'near'=4,'y'=4] {'x','core'}, dimensions={0} | all-to-all | bytes 1032192 | tf_op jit(solution)/shard_map/all_to_all | solution.py:229
  28.6 0.0 copy-done
  28.6 0.9 shard_map.41
  29.6 14.6 %all_to_all.26.parts_ref = bf16[16,88,128]{2,1,0:T(8,128)(2,1)S(1)} all-to-all(bf16[16,88,128]{2,1,0:T(8,128)(2,1)S(1)} %bitcast.7), channel_id=1, replica_groups={{0,4,8,12,1,5,9,13,2,6,10,14,3,7,11,15},{16,20,24,28,17,21,25,29,18,22,..., dimensions={0} | all-to-all | bytes 720896 | tf_op jit(solution)/shard_map/all_to_all | solution.py:216
  44.2 0.1 shard_map.42
  44.2 42.6 %all_to_all.27.parts_ref = bf16[8,88,128]{2,1,0:T(8,128)(2,1)S(1)} all-to-all(bf16[8,88,128]{2,1,0:T(8,128)(2,1)S(1)} %shard_map.42), channel_id=1, replica_groups={{0,32,64,96,16,48,80,112},{1,33,65,97,17,49,81,113},{2,34,66,98,18,50,8..., dimensions={0} | all-to-all | bytes 360448 | tf_op jit(solution)/shard_map/all_to_all | solution.py:216
  86.9 15.1 %all_to_all.28 = bf16[16,88,128]{2,1,0:T(8,128)(2,1)S(1)} all-to-all(bf16[16,88,128]{2,1,0:T(8,128)(2,1)S(1)} %shard_map.43), channel_id=1, replica_groups={{0,4,8,12,1,5,9,13,2,6,10,14,3,7,11,15},{16,20,24,28,17,21,25,29,18,22,..., dimensions={0} | all-to-all | bytes 720896 | tf_op jit(solution)/shard_map/all_to_all | solution.py:216
  102.0 2.8 %shard_map.44 = bf16[4,56,576]{2,1,0:T(8,128)(2,1)S(1)} custom-call(bf16[1408,128]{1,0:T(8,128)(2,1)S(1)} %bitcast.6, bf16[56,640]{1,0:T(8,128)(2,1)S(1)} %get-tuple-element.6.rows_ref), custom_call_target="tpu_custom_call" | custom-call | tf_op jit(solution)/shard_map/pallas_call | solution.py:205
  104.8 8.0 %all_to_all.29 = bf16[4,56,576]{2,1,0:T(8,128)(2,1)S(1)} all-to-all(bf16[4,56,576]{2,1,0:T(8,128)(2,1)S(1)} %shard_map.44), channel_id=1, replica_groups=mesh['x'=4,'core'=2,'block'=8,'near'=4,'y'=4] {'x'}, dimensions={0} | all-to-all | bytes 516096 | tf_op jit(solution)/shard_map/all_to_all | solution.py:239
  112.9 10.5 %all-gather = bf16[4,112,576]{2,1,0:T(8,128)(2,1)S(1)} all-gather(bf16[4,56,576]{2,1,0:T(8,128)(2,1)S(1)} %all_to_all.29), channel_id=2, replica_groups=mesh['x'=4,'core'=2,'block'=8,'near'=4,'y'=4] {'core'}, dimensions={1}, use_global_device_ids=true | all-gather | bytes 774144 | tf_op jit(solution)/shard_map/all_gather | solution.py:240
  123.4 0.8 copy.5
  (1 shorter events, 0.0 us)
Async XLA Ops:
  0.6 28.0 %copy-start = (f32[1,56,576]{2,1,0:T(8,128)S(1)}, f32[1,56,576]{2,1,0:T(8,128)}, u32[]{:S(2)}) copy-start(f32[1,56,576]{2,1,0:T(8,128)} %param.3) | copy-start | bytes 387076

commit v10 on v8

--- a/solution.py
+++ b/solution.py
@@ -96,7 +96,7 @@
 
     def put_both(i, j, tile):
         put(i, j, tile)
-        put(j, i, tile.T)
+        put(j, i, tile.astype(gram.dtype).T)
 
     corner = part(CORNER, HALF)
     block = jnp.where(col < HALF, corner, 0.0)
@@ -132,7 +132,7 @@
             block = product(slice(0, to), slice(start, stop))
             store[0:to, start:stop] = block.astype(store.dtype)
             if start:
-                store[start:stop, 0:start] = block[:start].T.astype(store.dtype)
+                store[start:stop, 0:start] = block[:start].astype(store.dtype).T
 
     rows = rows_ref[...]
     for store in (poly, work):
@@ -216,6 +216,7 @@
     rep, cluster = ("x", "core"), ("near", "y")
     blocks = lax.axis_size("block")
     members = lax.axis_size(cluster)
+    block_order = [*range(0, blocks, 2), *range(1, blocks, 2)]
     row_count, kv_width = momentum.shape[1:]
     factor = 0.2 * math.sqrt(max(row_count * blocks * members, kv_width))
 
@@ -224,7 +225,9 @@
 
     packed = packed.reshape(members, PACKED // members, TILE)
     packed = lax.all_to_all(packed, cluster, 0, 0, tiled=True)
-    packed = lax.all_to_all(total_of(packed, blocks), "block", 0, 0, tiled=True)
+    packed = lax.all_to_all(
+        total_of(packed, blocks), "block", 0, 0, axis_index_groups=[block_order], tiled=True
+    )
     packed = lax.all_to_all(total_of(packed, members), cluster, 0, 0, tiled=True)
     packed = packed.reshape(PACKED, TILE)
 

time: 126 us -> 124 us (0.984)
    all_to_all x1, blocking collectives: 45.4 us -> 40.8 us  [local(): lax.all_to_all(total_of(packed, blocks), 'block', 0, 0, axis_index_groups...]
    all_gather x1, blocking collectives: 7.02 us -> 9.66 us  [local(): update = lax.all_gather(update, 'core', axis=1)]
where the time goes in v10:
time: 124 us
  blocking collectives  119 us (96%)
  Pallas kernels  3.88 us (3%)
    all_to_all x1, blocking collectives, local(): lax.all_to_all(total_of(packed, blocks), 'block', 0, 0, axis_index_groups...  40.8 us
    all_to_all x1, blocking collectives, local(): received = lax.all_to_all(partial_grads[0], rep, 0, 0, tiled=True)  28 us
    all_to_all x1, blocking collectives, local(): lax.all_to_all(total_of(packed, members), cluster, 0, 0, tiled=True)  18.1 us
    all_to_all x1, blocking collectives, local(): packed = lax.all_to_all(packed, cluster, 0, 0, tiled=True)  14 us
    all_gather x1, blocking collectives, local(): update = lax.all_gather(update, 'core', axis=1)  9.66 us
    all_to_all x1, blocking collectives, local(): update = lax.all_to_all(update, 'x', 0, 0, tiled=True)  8.02 us
    pallas_call x1, Pallas kernels, newton(): pl.pallas_call(functools.partial(newton_kernel, factor), out_shape=bf16(r...  2.83 us

profile of v10, /device:TPU:1, one launch (start us, length us, event | category | flops | bytes accessed | tf_op | source)
XLA Modules:
  0.0 123.9 jit_solution(10162459023887856859)
XLA Ops:
  0.6 0.0 copy-start
  0.6 28.0 %all_to_all.25.received_ref = bf16[8,56,576]{2,1,0:T(8,128)(2,1)S(1)} all-to-all(bf16[8,56,576]{2,1,0:T(8,128)(2,1)} %bitcast.10), channel_id=1, replica_groups=mesh['x'=4,'core'=2,'block'=8,'near'=4,'y'=4] {'x','core'}, dimensions={0} | all-to-all | bytes 1032192 | tf_op jit(solution)/shard_map/all_to_all | solution.py:223
  28.6 0.0 copy-done
  28.6 0.9 shard_map.41
  29.6 14.0 %all_to_all.26.parts_ref = bf16[16,88,128]{2,1,0:T(8,128)(2,1)S(1)} all-to-all(bf16[16,88,128]{2,1,0:T(8,128)(2,1)S(1)} %bitcast.7), channel_id=1, replica_groups=mesh['x'=4,'core'=2,'block'=8,'near'=4,'y'=4] {'near','y'}, dimensions={0} | all-to-all | bytes 720896 | tf_op jit(solution)/shard_map/all_to_all | solution.py:227
  43.6 0.1 shard_map.42
  43.6 40.8 %all_to_all.27.parts_ref = bf16[8,88,128]{2,1,0:T(8,128)(2,1)S(1)} all-to-all(bf16[8,88,128]{2,1,0:T(8,128)(2,1)S(1)} %shard_map.42), channel_id=1, replica_groups={{0,32,64,96,16,48,80,112},{1,33,65,97,17,49,81,113},{2,34,66,98,18,50,8..., dimensions={0} | all-to-all | bytes 360448 | tf_op jit(solution)/shard_map/all_to_all | solution.py:228
  84.4 18.1 %all_to_all.28 = bf16[16,88,128]{2,1,0:T(8,128)(2,1)S(1)} all-to-all(bf16[16,88,128]{2,1,0:T(8,128)(2,1)S(1)} %shard_map.43), channel_id=1, replica_groups=mesh['x'=4,'core'=2,'block'=8,'near'=4,'y'=4] {'near','y'}, dimensions={0} | all-to-all | bytes 720896 | tf_op jit(solution)/shard_map/all_to_all | solution.py:231
  102.6 2.8 %shard_map.44 = bf16[4,56,576]{2,1,0:T(8,128)(2,1)S(1)} custom-call(bf16[1408,128]{1,0:T(8,128)(2,1)S(1)} %bitcast.6, bf16[56,640]{1,0:T(8,128)(2,1)S(1)} %get-tuple-element.6.rows_ref), custom_call_target="tpu_custom_call" | custom-call | tf_op jit(solution)/shard_map/pallas_call | solution.py:205
  105.4 8.0 %all_to_all.29 = bf16[4,56,576]{2,1,0:T(8,128)(2,1)S(1)} all-to-all(bf16[4,56,576]{2,1,0:T(8,128)(2,1)S(1)} %shard_map.44), channel_id=1, replica_groups=mesh['x'=4,'core'=2,'block'=8,'near'=4,'y'=4] {'x'}, dimensions={0} | all-to-all | bytes 516096 | tf_op jit(solution)/shard_map/all_to_all | solution.py:235
  113.4 9.7 %all-gather = bf16[4,112,576]{2,1,0:T(8,128)(2,1)S(1)} all-gather(bf16[4,56,576]{2,1,0:T(8,128)(2,1)S(1)} %all_to_all.29), channel_id=2, replica_groups=mesh['x'=4,'core'=2,'block'=8,'near'=4,'y'=4] {'core'}, dimensions={1}, use_global_device_ids=true | all-gather | bytes 774144 | tf_op jit(solution)/shard_map/all_gather | solution.py:236
  123.1 0.8 copy.5
  (1 shorter events, 0.0 us)
Async XLA Ops:
  0.6 28.0 %copy-start = (f32[1,56,576]{2,1,0:T(8,128)S(1)}, f32[1,56,576]{2,1,0:T(8,128)}, u32[]{:S(2)}) copy-start(f32[1,56,576]{2,1,0:T(8,128)} %param.3) | copy-start | bytes 387076

commit v11 on v10

--- a/solution.py
+++ b/solution.py
@@ -216,7 +216,7 @@
     rep, cluster = ("x", "core"), ("near", "y")
     blocks = lax.axis_size("block")
     members = lax.axis_size(cluster)
-    block_order = [*range(0, blocks, 2), *range(1, blocks, 2)]
+    block_order = sorted(range(blocks), key=lambda block: (block // 2 % 2, block))
     row_count, kv_width = momentum.shape[1:]
     factor = 0.2 * math.sqrt(max(row_count * blocks * members, kv_width))
 

time: 124 us -> 125 us (level)
  no operation moved by 1% of the time
where the time goes in v11:
time: 125 us
  blocking collectives  120 us (96%)
  Pallas kernels  3.87 us (3%)
    all_to_all x1, blocking collectives, local(): lax.all_to_all(total_of(packed, blocks), 'block', 0, 0, axis_index_groups...  40.6 us
    all_to_all x1, blocking collectives, local(): received = lax.all_to_all(partial_grads[0], rep, 0, 0, tiled=True)  28 us
    all_to_all x1, blocking collectives, local(): lax.all_to_all(total_of(packed, members), cluster, 0, 0, tiled=True)  18.2 us
    all_to_all x1, blocking collectives, local(): packed = lax.all_to_all(packed, cluster, 0, 0, tiled=True)  14 us
    all_gather x1, blocking collectives, local(): update = lax.all_gather(update, 'core', axis=1)  10.8 us
    all_to_all x1, blocking collectives, local(): update = lax.all_to_all(update, 'x', 0, 0, tiled=True)  8.02 us
    pallas_call x1, Pallas kernels, newton(): pl.pallas_call(functools.partial(newton_kernel, factor), out_shape=bf16(r...  2.83 us

profile of v11, /device:TPU:1, one launch (start us, length us, event | category | flops | bytes accessed | tf_op | source)
XLA Modules:
  0.0 124.9 jit_solution(15970616066063478424)
XLA Ops:
  0.6 0.0 copy-start
  0.6 28.0 %all_to_all.25.received_ref = bf16[8,56,576]{2,1,0:T(8,128)(2,1)S(1)} all-to-all(bf16[8,56,576]{2,1,0:T(8,128)(2,1)} %bitcast.10), channel_id=1, replica_groups=mesh['x'=4,'core'=2,'block'=8,'near'=4,'y'=4] {'x','core'}, dimensions={0} | all-to-all | bytes 1032192 | tf_op jit(solution)/shard_map/all_to_all | solution.py:223
  28.6 0.0 copy-done
  28.6 0.9 shard_map.41
  29.6 14.0 %all_to_all.26.parts_ref = bf16[16,88,128]{2,1,0:T(8,128)(2,1)S(1)} all-to-all(bf16[16,88,128]{2,1,0:T(8,128)(2,1)S(1)} %bitcast.7), channel_id=1, replica_groups=mesh['x'=4,'core'=2,'block'=8,'near'=4,'y'=4] {'near','y'}, dimensions={0} | all-to-all | bytes 720896 | tf_op jit(solution)/shard_map/all_to_all | solution.py:227
  43.6 0.1 shard_map.42
  43.6 40.6 %all_to_all.27.parts_ref = bf16[8,88,128]{2,1,0:T(8,128)(2,1)S(1)} all-to-all(bf16[8,88,128]{2,1,0:T(8,128)(2,1)S(1)} %shard_map.42), channel_id=1, replica_groups={{0,16,64,80,32,48,96,112},{1,17,65,81,33,49,97,113},{2,18,66,82,34,50,9..., dimensions={0} | all-to-all | bytes 360448 | tf_op jit(solution)/shard_map/all_to_all | solution.py:228
  84.3 18.2 %all_to_all.28 = bf16[16,88,128]{2,1,0:T(8,128)(2,1)S(1)} all-to-all(bf16[16,88,128]{2,1,0:T(8,128)(2,1)S(1)} %shard_map.43), channel_id=1, replica_groups=mesh['x'=4,'core'=2,'block'=8,'near'=4,'y'=4] {'near','y'}, dimensions={0} | all-to-all | bytes 720896 | tf_op jit(solution)/shard_map/all_to_all | solution.py:231
  102.4 2.8 %shard_map.44 = bf16[4,56,576]{2,1,0:T(8,128)(2,1)S(1)} custom-call(bf16[1408,128]{1,0:T(8,128)(2,1)S(1)} %bitcast.6, bf16[56,640]{1,0:T(8,128)(2,1)S(1)} %get-tuple-element.6.rows_ref), custom_call_target="tpu_custom_call" | custom-call | tf_op jit(solution)/shard_map/pallas_call | solution.py:205
  105.3 8.0 %all_to_all.29 = bf16[4,56,576]{2,1,0:T(8,128)(2,1)S(1)} all-to-all(bf16[4,56,576]{2,1,0:T(8,128)(2,1)S(1)} %shard_map.44), channel_id=1, replica_groups=mesh['x'=4,'core'=2,'block'=8,'near'=4,'y'=4] {'x'}, dimensions={0} | all-to-all | bytes 516096 | tf_op jit(solution)/shard_map/all_to_all | solution.py:235
  113.3 10.8 %all-gather = bf16[4,112,576]{2,1,0:T(8,128)(2,1)S(1)} all-gather(bf16[4,56,576]{2,1,0:T(8,128)(2,1)S(1)} %all_to_all.29), channel_id=2, replica_groups=mesh['x'=4,'core'=2,'block'=8,'near'=4,'y'=4] {'core'}, dimensions={1}, use_global_device_ids=true | all-gather | bytes 774144 | tf_op jit(solution)/shard_map/all_gather | solution.py:236
  124.0 0.8 copy.5
  (1 shorter events, 0.0 us)
Async XLA Ops:
  0.6 28.0 %copy-start = (f32[1,56,576]{2,1,0:T(8,128)S(1)}, f32[1,56,576]{2,1,0:T(8,128)}, u32[]{:S(2)}) copy-start(f32[1,56,576]{2,1,0:T(8,128)} %param.3) | copy-start | bytes 387076
